TPU v7x, 256 devices: a whole 4x4x8 slice. The times are simulated.
256 devices in a mesh: expert: 64 (over z, x, core), dp: 4 (over y).
Axes of the slice: x: 4, y: 4, z: 8, core: 2. Of those that a mesh axis runs over, the one named last changes fastest.
Arguments:
- features: bfloat16 [32768, 32, 64], P(('expert', 'dp')), may hold values from -1 to 1
- spacing: float32 [32768, 32], P(('expert', 'dp')), may hold values from 0.02 to 0.3
- targets: float32 [3, 32768], P(None, ('expert', 'dp')), may hold values from 0 to 1
- ray_length: int32 [32768], P(('expert', 'dp')), may hold values from 1 to 32, as said below
- cell_id: int32 [32768, 32], P(('expert', 'dp')), may hold values from 0 to 127, as said below
- slot_rank: int32 [32768, 32], P(('expert', 'dp')), may hold values from -1 to 47, as said below
- image_id: int32 [32768], P(('expert', 'dp')), may hold values from 0 to 4095, as said below
- params: float32 [128, 848, 256], P('expert'), may hold values from -5 to 5
- first_moment: float32 [128, 848, 256], P('expert'), may hold values from -0.75 to 0.75
- second_moment: float32 [128, 848, 256], P('expert'), may hold values from 1e-06 to 0.01
- code_table: float32 [4096, 64], P(('expert', 'dp')), may hold values from -6 to 6
- table_first: float32 [4096, 64], P(('expert', 'dp')), may hold values from -0.75 to 0.75
- table_second: float32 [4096, 64], P(('expert', 'dp')), may hold values from 1e-06 to 0.01
Outputs:
- ray_loss: float32 [32768], P(('expert', 'dp'))
- new_params: float32 [128, 848, 256], P('expert')
- new_first_moment: float32 [128, 848, 256], P('expert')
- new_second_moment: float32 [128, 848, 256], P('expert')
- new_code_table: float32 [4096, 64], P(('expert', 'dp'))
- new_table_first: float32 [4096, 64], P(('expert', 'dp'))
- new_table_second: float32 [4096, 64], P(('expert', 'dp'))
Inputs may be any that keep to these rules, and one draw needn't show every extreme that they name: `ray_length`: rays form aligned blocks of 128, one a device, in the order of the axes expert then dp. In every block the lengths sum to 3072 and some ray has all 32 samples. `cell_id`: also given for samples at or beyond their ray's length, where it is unused. `slot_rank`: for a sample below its ray's length: its rank among the live samples of its block of 128 rays that have the same cell_id, counted ray by ray and along each ray; -1 for the other samples. No block has more than 48 live samples of one cell_id; in every block some cell_id has exactly 48, and one cell_id has 48 in every block. `image_id`: A ray of block b names an image from b * 16 to (b + 1) * 16 - 1.
All inputs are finite; a program needn't handle non-finite values.
Results may differ from a plain program's by a relative error of at most 0.0046.
Values may be sent and summed in bfloat16 or wider, within the bound.
No kernel may reach another device: no remote copies, remote signals or barrier semaphores. Data moves between devices by JAX's collectives and lax.ppermute only.
A program may use at most 128 MiB of HBM per device.

v0:
```python
import jax
import jax.numpy as jnp
from jax import lax
from jax.sharding import PartitionSpec as P

NET_WIDTH = 256
CODE_WIDTH = 64
ENC_WIDTH = 64
LAYERS = 4
SAMPLES = 32


BETA_ONE = 0.9
BETA_TWO = 0.999
LEARN_RATE = 0.001
ADAM_EPS = 1e-08
CORRECT_ONE = 1.0 - 0.9**10
CORRECT_TWO = 1.0 - 0.999**10


def adam_update(param_now, gradient, moment_one, moment_two):
    new_one = BETA_ONE * moment_one + (1.0 - BETA_ONE) * gradient
    new_two = BETA_TWO * moment_two + (1.0 - BETA_TWO) * gradient * gradient
    update = LEARN_RATE * (new_one / CORRECT_ONE) / (jnp.sqrt(new_two / CORRECT_TWO) + ADAM_EPS)
    return (param_now - update, new_one, new_two)


def composite(raw_out, spacing, live_mask, targets):
    density = jax.nn.softplus(raw_out[0])
    colors = jax.nn.sigmoid(raw_out[1:4])
    optical = density * spacing * live_mask
    before = jnp.cumsum(optical, axis=1) - optical
    weight = jnp.exp(-before) * (1.0 - jnp.exp(-optical))
    render = jnp.sum(weight[None] * colors, axis=2)
    return 0.5 * jnp.sum((render - targets) ** 2, axis=0)


def place_rows(rows, slot_index, slots_all):
    blank = jnp.zeros((slots_all,) + rows.shape[1:], rows.dtype)
    return blank.at[slot_index].set(rows, mode="drop")


def pick_rows(buffer, slot_index):
    return jnp.take(buffer, slot_index, axis=0, mode="fill", fill_value=0)


def hidden_pass(weights_bf, inputs):
    head_row = ENC_WIDTH + (LAYERS - 1) * NET_WIDTH
    activations = [inputs]
    preacts = []
    current = inputs
    row_start = 0
    row_count = ENC_WIDTH
    for layer_index in range(LAYERS):
        matrix = weights_bf[:, row_start : row_start + row_count, :]
        bias_row = weights_bf[:, head_row + 9 + layer_index, :].astype(jnp.float32)
        preact = (
            jnp.einsum("enr,erw->enw", current, matrix, preferred_element_type=jnp.float32)
            + bias_row[:, None, :]
        )
        current = jnp.maximum(preact, 0.0).astype(jnp.bfloat16)
        preacts.append(preact)
        activations.append(current)
        row_start = row_start + row_count
        row_count = NET_WIDTH
    return (activations, preacts)


def hidden_grads(weights_bf, activations, preacts, upstream):
    weight_grads = [None] * LAYERS
    bias_grads = [None] * LAYERS
    for layer_index in reversed(range(LAYERS)):
        pre_grad = jnp.where(preacts[layer_index] > 0, upstream, 0.0).astype(jnp.bfloat16)
        weight_grads[layer_index] = jnp.einsum(
            "enr,enw->erw", activations[layer_index], pre_grad, preferred_element_type=jnp.float32
        )
        bias_grads[layer_index] = jnp.sum(pre_grad, axis=1, dtype=jnp.float32)
        if layer_index > 0:
            row_start = ENC_WIDTH + (layer_index - 1) * NET_WIDTH
            upstream = jnp.einsum(
                "enw,erw->enr",
                pre_grad,
                weights_bf[:, row_start : row_start + NET_WIDTH, :],
                preferred_element_type=jnp.float32,
            )
    return (weight_grads, bias_grads)


def assemble(weight_grads, bias_grads, hidden_grad, code_grad_head, bias_grad_head):
    held_count = hidden_grad.shape[0]
    pieces = list(weight_grads) + [
        hidden_grad,
        jnp.pad(code_grad_head, ((0, 0), (0, 0), (0, NET_WIDTH - CODE_WIDTH))),
        jnp.pad(bias_grad_head, ((0, 0), (0, NET_WIDTH - 4)))[:, None, :],
        jnp.stack(bias_grads, axis=1),
        jnp.zeros((held_count, 7 - LAYERS, NET_WIDTH), jnp.float32),
    ]
    return jnp.concatenate(pieces, axis=1)


def shards(
    features,
    spacing,
    targets,
    ray_length,
    cell_id,
    slot_rank,
    image_id,
    params,
    first_moment,
    second_moment,
    code_table,
    table_first,
    table_second,
):
    ray_rows = features.shape[0]
    sample_count = ray_rows * SAMPLES
    groups = lax.axis_size("expert")
    held_count = params.shape[0]
    experts_all = held_count * groups
    capacity = 2 * (sample_count * 3 // 4 // experts_all)
    slots_all = experts_all * capacity
    head_row = ENC_WIDTH + (LAYERS - 1) * NET_WIDTH
    weights_bf = params.astype(jnp.bfloat16)
    table_rows = code_table.shape[0]
    block_index = lax.axis_index("expert") * lax.axis_size("dp") + lax.axis_index("dp")
    local_image = image_id - block_index * table_rows
    picker = (local_image[:, None] == jnp.arange(table_rows, dtype=jnp.int32)[None, :]).astype(
        jnp.bfloat16
    )
    ray_code = jnp.dot(
        picker, code_table.astype(jnp.bfloat16), preferred_element_type=jnp.float32
    ).astype(jnp.bfloat16)
    position = jnp.arange(SAMPLES, dtype=jnp.int32)
    live_mask = (position[None, :] < ray_length[:, None]).astype(jnp.float32)
    flat_rank = slot_rank.reshape(sample_count)
    slot_index = jnp.where(
        flat_rank >= 0, cell_id.reshape(sample_count) * capacity + flat_rank, slots_all
    )
    positions = features.reshape(sample_count, ENC_WIDTH)
    sample_code = jnp.broadcast_to(ray_code[:, None, :], (ray_rows, SAMPLES, CODE_WIDTH)).reshape(
        sample_count, CODE_WIDTH
    )
    outgoing = place_rows(
        jnp.concatenate([positions, sample_code], axis=1), slot_index, slots_all
    ).reshape(experts_all, capacity, ENC_WIDTH + CODE_WIDTH)
    arrived = lax.all_to_all(outgoing, "expert", split_axis=0, concat_axis=1, tiled=True)
    hidden_head = weights_bf[:, head_row : head_row + 4, :]
    inputs = arrived[:, :, :ENC_WIDTH]
    code_rows = arrived[:, :, ENC_WIDTH:]
    activations, preacts = hidden_pass(weights_bf, inputs)
    raw_out = jnp.einsum(
        "enw,ecw->enc", activations[-1], hidden_head, preferred_element_type=jnp.float32
    )
    code_head = weights_bf[:, head_row + 4 : head_row + 8, :CODE_WIDTH]
    raw_out = raw_out + jnp.einsum(
        "enk,eck->enc", code_rows, code_head, preferred_element_type=jnp.float32
    )
    raw_out = raw_out + weights_bf[:, head_row + 8, :4].astype(jnp.float32)[:, None, :]
    returned = lax.all_to_all(raw_out, "expert", split_axis=1, concat_axis=0, tiled=True)
    raw_samples = pick_rows(returned.reshape(slots_all, 4), slot_index)
    raw_grid = raw_samples.T.reshape(4, ray_rows, SAMPLES)

    def loss_of(raw_in):
        return composite(raw_in, spacing, live_mask, targets)

    ray_loss, pullback = jax.vjp(loss_of, raw_grid)
    (raw_grad,) = pullback(jnp.ones_like(ray_loss))
    cotangent = raw_grad.reshape(4, sample_count).T.astype(jnp.bfloat16)
    cot_slots = place_rows(cotangent, slot_index, slots_all).reshape(experts_all, capacity, 4)
    cot_in = lax.all_to_all(cot_slots, "expert", split_axis=0, concat_axis=1, tiled=True)
    upstream = jnp.einsum("enc,ecw->enw", cot_in, hidden_head, preferred_element_type=jnp.float32)
    weight_grads, bias_grads = hidden_grads(weights_bf, activations, preacts, upstream)
    hidden_grad = jnp.einsum(
        "enc,enw->ecw", cot_in, activations[-1], preferred_element_type=jnp.float32
    )
    code_grad_head = jnp.einsum(
        "enc,enk->eck", cot_in, code_rows, preferred_element_type=jnp.float32
    )
    bias_grad_head = jnp.sum(cot_in, axis=1, dtype=jnp.float32)
    code_back = jnp.einsum("enc,eck->enk", cot_in, code_head, preferred_element_type=jnp.float32)
    code_back = code_back.reshape(held_count, groups * capacity // 2, 2 * CODE_WIDTH)
    code_slot_grad = lax.all_to_all(
        code_back, "expert", split_axis=1, concat_axis=0, tiled=True
    ).reshape(slots_all, CODE_WIDTH)
    local_grad = assemble(weight_grads, bias_grads, hidden_grad, code_grad_head, bias_grad_head)
    param_grad = lax.psum(local_grad, "dp")
    sample_code_grad = pick_rows(code_slot_grad, slot_index).reshape(ray_rows, SAMPLES, CODE_WIDTH)
    ray_code_grad = jnp.sum(sample_code_grad, axis=1)
    table_grad = lax.dot_general(
        picker.astype(jnp.float32),
        ray_code_grad,
        (((0,), (0,)), ((), ())),
        precision=lax.Precision.HIGHEST,
        preferred_element_type=jnp.float32,
    )
    new_params, new_first, new_second = adam_update(params, param_grad, first_moment, second_moment)
    new_table, new_table_first, new_table_second = adam_update(
        code_table, table_grad, table_first, table_second
    )
    return (
        ray_loss,
        new_params,
        new_first,
        new_second,
        new_table,
        new_table_first,
        new_table_second,
    )


def solution(mesh):
    return jax.shard_map(
        shards,
        mesh=mesh,
        in_specs=(
            P(("expert", "dp"), None, None),
            P(("expert", "dp"), None),
            P(None, ("expert", "dp")),
            P(("expert", "dp")),
            P(("expert", "dp"), None),
            P(("expert", "dp"), None),
            P(("expert", "dp")),
            P("expert", None, None),
            P("expert", None, None),
            P("expert", None, None),
            P(("expert", "dp"), None),
            P(("expert", "dp"), None),
            P(("expert", "dp"), None),
        ),
        out_specs=(
            P(("expert", "dp")),
            P("expert", None, None),
            P("expert", None, None),
            P("expert", None, None),
            P(("expert", "dp"), None),
            P(("expert", "dp"), None),
            P(("expert", "dp"), None),
        ),
        check_vma=False,
    )
```

profile of v0, /device:TPU:2, one launch (start us, length us, event | category | flops | bytes accessed | tf_op | source)
XLA Modules:
  0.0 318.6 jit_solution(14110664779036031382)
XLA Ops:
  7.2 0.7 broadcast_subtract_fusion
  7.8 0.9 convolution_convert_fusion
  8.9 0.8 compare_and_fusion
  9.9 2.5 copy.100
  12.3 1.1 broadcast_in_dim.78
  13.4 13.5 %scatter_custom_fusion = bf16[6144,128]{1,0:T(8,128)(2,1)} fusion(s32[4096]{0:T(1024)S(1)} %bitcast.84, bf16[4096,64]{1,0:T(8,128)(2,1)} %bitcast.78, bf16[]{:T(256)} %constant.125, bf16[4096,64]{1,0:T(8,128)(2,1)S(1)} %bitcast.77, bf16[]{:T(256)} %constant.35.clone.1), kind=kCustom, calls=%fused_computation.44 | custom fusion | flops 2097152 | bytes 3145732 | tf_op jit(solution)/shard_map/scatter | solution.py:40
  26.9 12.7 %all-to-all-start = ((bf16[128,48,128]{2,1,0:T(8,128)(2,1)}), bf16[128,48,128]{2,1,0:T(8,128)(2,1)S(1)}, u32[]{:S(2)}, u32[]{:S(2)}) async-start(bf16[128,48,128]{2,1,0:T(8,128)(2,1)} %bitcast.74), calls=%async_computation | async-start | bytes 3145728 | tf_op jit(solution)/shard_map/all_to_all | solution.py:147
  39.9 0.8 copy-done.10
  40.7 38.8 %all-to-all-done = bf16[128,48,128]{2,1,0:T(8,128)(2,1)S(1)} async-done(((bf16[128,48,128]{2,1,0:T(8,128)(2,1)}), bf16[128,48,128]{2,1,0:T(8,128)(2,1)S(1)}, u32[]{:S(2)}, u32[]{:S(2)}) %all-to-all-start) | async-done | bytes 1572896 | tf_op jit(solution)/shard_map/all_to_all | solution.py:147
  79.6 2.0 fusion.2
  81.7 3.1 fusion.3
  84.8 3.1 fusion.4
  87.9 3.1 fusion.5
  91.0 0.9 fusion.24
  91.9 1.7 copy-done.3
  94.2 2.9 copy.105
  97.1 5.6 %reshape.184 = f32[64,1,384]{2,1,0:T(1,128)} reshape(f32[3072,2,4]{2,1,0:T(2,128)S(1)} %bitcast.71) | data formatting | bytes 196608
  102.7 5.7 %all-to-all-start.1 = ((f32[64,1,384]{2,1,0:T(1,128)}), f32[64,1,384]{2,1,0:T(1,128)S(1)}, u32[]{:S(2)}, u32[]{:S(2)}) async-start(f32[64,1,384]{2,1,0:T(1,128)} %reshape.184), calls=%async_computation.1 | async-start | bytes 196608 | tf_op jit(solution)/shard_map/all_to_all | solution.py:160
  108.5 9.3 %all-to-all-done.1 = f32[64,1,384]{2,1,0:T(1,128)S(1)} async-done(((f32[64,1,384]{2,1,0:T(1,128)}), f32[64,1,384]{2,1,0:T(1,128)S(1)}, u32[]{:S(2)}, u32[]{:S(2)}) %all-to-all-start.1) | async-done | bytes 98336 | tf_op jit(solution)/shard_map/all_to_all | solution.py:160
  118.3 0.9 reduce.14
  119.2 6.6 %reshape.185 = f32[3072,2,4]{2,1,0:T(2,128)} reshape(f32[64,384]{1,0:T(8,128)S(1)} %reduce.14) | data formatting | bytes 196608
  125.7 2.1 copy.141
  127.9 14.1 %gather_fusion = f32[4096,4]{1,0:T(8,128)} fusion(f32[6144,4]{1,0:T(8,128)S(1)} %bitcast.62, s32[4096]{0:T(1024)S(1)} %broadcast_clamp_fusion), kind=kCustom, calls=%fused_computation | custom fusion | bytes 147456 | tf_op jit(solution)/shard_map/jit(_take)/gather | solution.py:44
  141.9 2.2 copy.108
  146.4 11.4 %scatter_custom_fusion.1 = bf16[6144,4]{1,0:T(8,128)(2,1)S(1)} fusion(s32[4096]{0:T(1024)S(1)} %bitcast.86, bf16[4096,4]{1,0:T(8,128)(2,1)S(1)} %copy.123, bf16[]{:T(256)} %constant.35.clone.1), kind=kCustom, calls=%fused_computation.56 | custom fusion | bytes 49154 | tf_op jit(solution)/shard_map/scatter | solution.py:40
  157.8 1.0 copy.124
  159.0 14.1 %all_to_all.66 = bf16[64,2,192]{2,1,0:T(2,128)(2,1)S(1)} all-to-all(bf16[64,2,192]{2,1,0:T(2,128)(2,1)S(1)} %reshape.186), channel_id=1, replica_groups=mesh['expert'=64,'dp'=4] {'expert'}, dimensions={0} | all-to-all | bytes 98304 | tf_op jit(solution)/shard_map/all_to_all | solution.py:171
  173.8 3.6 %fusion.23 = f32[2,4,256]{2,1,0:T(4,128)S(1)} fusion(bf16[2,3072,4]{1,2,0:T(4,128)(2,1)S(1)} %all_to_all.58, f32[2,3072,256]{2,1,0:T(8,128)} %copy-done.3, f32[2,256]{1,0:T(2,128)S(1)} %bitcast.89), kind=kOutput, calls=%fused_computation.54 | convolution fusion | flops 17301504 | bytes 6350848 | tf_op jit(solution)/shard_map/enc,enw->ecw/dot_general | solution.py:174
  177.9 2.4 fusion.51
  180.5 2.8 convert_reduce_fusion
  183.3 2.3 fusion.21
  185.6 1.4 convert_reduce_fusion.1
  187.3 2.3 fusion.19
  189.6 1.4 convert_reduce_fusion.2
  191.0 4.3 %convert_reduce_fusion.3 = (f32[2,256]{1,0:T(2,128)S(1)}, bf16[2,3072,256]{2,1,0:T(8,128)(2,1)}) fusion(bf16[2,3072,256]{2,1,0:T(8,128)(2,1)S(1)} %get-tuple-element.32, bf16[2,848,256]{2,1,0:T(8,128)(2,1)} %copy-done.10, u8[3072,256]{1,0:T(8,128)(4,1)S(1)} %copy-done.15), kind=kOutput, calls=%fused_computation.16 | convolution fusion | flops 817888768 | bytes 7342080 | tf_op jit(solution)/shard_map/enw,erw->enr/dot_general | solution.py:80
  195.3 1.5 reshape.134
  196.7 7.2 %copy.133 = f32[2,1536,128]{2,0,1:T(2,128)} copy(f32[2,1536,128]{2,1,0:T(8,128)} %reshape.134) | data formatting | bytes 3145728 | tf_op jit(solution)/shard_map/reshape | solution.py:182
  204.0 5.6 %all-to-all-start.3 = ((f32[2,1536,128]{2,0,1:T(2,128)}), f32[2,1536,128]{2,0,1:T(2,128)S(1)}, u32[]{:S(2)}, u32[]{:S(2)}) async-start(f32[2,1536,128]{2,0,1:T(2,128)} %copy.133), calls=%async_computation.3 | async-start | bytes 3145728 | tf_op jit(solution)/shard_map/all_to_all | solution.py:183
  209.7 2.8 fusion.11
  212.5 5.1 %fusion.17 = f32[2,256,256]{2,1,0:T(8,128)} fusion(bf16[2,3072,256]{2,1,0:T(8,128)(2,1)S(1)} %copy-done.14, f32[2,3072,256]{2,1,0:T(8,128)} %copy-done, f32[2,256]{1,0:T(2,128)S(1)} %bitcast.92), kind=kOutput, calls=%fused_computation.48 | convolution fusion | flops 810024960 | bytes 9963520 | tf_op jit(solution)/shard_map/enr,enw->erw/dot_general | solution.py:74
  217.6 7.2 %concatenate.7 = f32[2,848,256]{2,1,0:T(8,128)} concatenate(f32[2,64,256]{2,1,0:T(8,128)S(1)} %fusion.11, f32[2,256,256]{2,1,0:T(8,128)} %fusion.17, f32[2,256,256]{2,1,0:T(8,128)} %fusion.19, f32[2,256,256]{2,1,0:T(8,128)} %fusion.21, f32[2,4,256]{2,1,0:T(4,128)S(1)} %fusion.23, f32[2,4,256]{2,1,0:T(4,128)S(1)} %pad.16, f32[2,1,256]{2,1,0:T(1,128)S(1)} %broadcast_in_dim.84, ...), dimensions={1} | concatenate | bytes 3473408 | tf_op jit(solution)/shard_map/concatenate | solution.py:98
  225.4 58.9 %all-reduce.6.cloned.1.call-done = f32[2,848,256]{2,1,0:T(8,128)} async-done(((f32[2,848,256]{2,1,0:T(8,128)}), f32[2,848,256]{2,1,0:T(8,128)}) %all-reduce.6.cloned.1.call-update) | async-done | bytes 1736720 | tf_op jit(solution)/shard_map/psum | solution.py:187
  284.3 5.5 %divide_subtract_fusion = (f32[2,848,256]{2,1,0:T(8,128)}, f32[2,848,256]{2,1,0:T(8,128)}, f32[2,848,256]{2,1,0:T(8,128)}) fusion(f32[2,848,256]{2,1,0:T(8,128)S(1)} %copy-done.9, f32[2,848,256]{2,1,0:T(8,128)} %all-reduce.6.cloned.1.call-done, f32[2,848,256]{2,1,0:T(8,128)} %param.21, f32[2,848,256]{2,1,0:T(8,128)} %param.22), kind=kLoop, calls=%fused_computation.30 | loop fusion | flops 5210112 | bytes 12156928 | tf_op jit(solution)/shard_map/sub | solution.py:25
  289.9 1.3 copy.135
  291.2 2.4 reshape.135
  293.6 14.1 %gather_fusion.1 = f32[4096,64]{1,0:T(8,128)} fusion(f32[6144,64]{1,0:T(8,128)S(1)} %reshape.135, s32[4096]{0:T(1024)S(1)} %broadcast_clamp_fusion), kind=kCustom, calls=%fused_computation.1 | custom fusion | bytes 2113536 | tf_op jit(solution)/shard_map/jit(_take)/gather | solution.py:44
  307.7 2.8 select_reduce_fusion
  310.6 0.9 divide_subtract_fusion.1
  (119 shorter events, 6.6 us)
Async XLA Ops:
  13.4 26.2 %copy-start.8 = (f32[2,848,256]{2,1,0:T(8,128)S(1)}, f32[2,848,256]{2,1,0:T(8,128)}, u32[]{:S(2)}) copy-start(f32[2,848,256]{2,1,0:T(8,128)} %param.20) | copy-start | bytes 5210116
  26.9 52.6 %all-to-all-start = ((bf16[128,48,128]{2,1,0:T(8,128)(2,1)}), bf16[128,48,128]{2,1,0:T(8,128)(2,1)S(1)}, u32[]{:S(2)}, u32[]{:S(2)}) async-start(bf16[128,48,128]{2,1,0:T(8,128)(2,1)} %bitcast.74), calls=%async_computation | async-start | bytes 3145728 | tf_op jit(solution)/shard_map/all_to_all | solution.py:147
  39.8 0.9 copy-start.10
  40.7 38.9 %copy-start.11 = (bf16[2,848,256]{2,1,0:T(8,128)(2,1)S(1)}, bf16[2,848,256]{2,1,0:T(8,128)(2,1)}, u32[]{:S(2)}) copy-start(bf16[2,848,256]{2,1,0:T(8,128)(2,1)} %copy-done.10) | copy-start | bytes 2605060
  79.6 14.0 %copy-start.4 = (bf16[2,64,48,128]{3,2,1,0:T(8,128)(2,1)}, bf16[2,64,48,128]{3,2,1,0:T(8,128)(2,1)S(1)}, u32[]{:S(2)}) copy-start(bf16[2,64,48,128]{3,2,1,0:T(8,128)(2,1)S(1)} %copy.102) | copy-start | bytes 4718596
  81.7 3.1 copy-start
  84.8 3.1 copy-start.1
  87.9 3.2 copy-start.2
  91.0 2.6 copy-start.3
  102.7 15.0 %all-to-all-start.1 = ((f32[64,1,384]{2,1,0:T(1,128)}), f32[64,1,384]{2,1,0:T(1,128)S(1)}, u32[]{:S(2)}, u32[]{:S(2)}) async-start(f32[64,1,384]{2,1,0:T(1,128)} %reshape.184), calls=%async_computation.1 | async-start | bytes 196608 | tf_op jit(solution)/shard_map/all_to_all | solution.py:160
  127.8 16.6 %copy-start.18 = (f32[128,32]{0,1:T(8,128)S(1)}, f32[128,32]{0,1:T(8,128)}, u32[]{:S(2)}) copy-start(f32[128,32]{0,1:T(8,128)} %param.14) | copy-start | bytes 49156
  127.9 16.6 %copy-start.22 = (s32[128]{0:T(128)S(1)}, s32[128]{0:T(128)}, u32[]{:S(2)}) copy-start(s32[128]{0:T(128)} %param.16) | copy-start | bytes 1540
  141.9 2.9 copy-start.23
  173.7 3.6 %copy-start.5 = (bf16[2,64,48,128]{3,2,1,0:T(8,128)(2,1)S(1)}, bf16[2,64,48,128]{3,2,1,0:T(8,128)(2,1)}, u32[]{:S(2)}) copy-start(bf16[2,64,48,128]{3,2,1,0:T(8,128)(2,1)} %copy-done.4) | copy-start | bytes 4718596
  173.7 4.2 %copy-start.12 = (bf16[2,848,256]{2,1,0:T(8,128)(2,1)S(1)}, bf16[2,848,256]{2,1,0:T(8,128)(2,1)}, u32[]{:S(2)}) copy-start(bf16[2,848,256]{2,1,0:T(8,128)(2,1)} %copy-done.10) | copy-start | bytes 2605060
  177.9 5.3 %slice-start.2 = ((s8[6291456]{0:T(1024)(128)(4,1)}), s8[2097152]{0:T(1024)(128)(4,1)S(1)}, s32[]{:S(2)}) async-start(s8[6291456]{0:T(1024)(128)(4,1)} %bitcast.65), calls=%async_computation.7 | async-start | bytes 4194304
  180.5 2.8 slice-start.3
  183.3 2.4 copy-start.17
  183.3 3.7 %slice-start = ((s8[6291456]{0:T(1024)(128)(4,1)}), s8[4194304]{0:T(1024)(128)(4,1)S(1)}, s32[]{:S(2)}) async-start(s8[6291456]{0:T(1024)(128)(4,1)} %bitcast.63), calls=%async_computation.5 | async-start | bytes 8388608
  185.6 1.6 slice-start.1
  187.3 2.3 copy-start.16
  189.6 1.4 copy-start.15
  191.0 4.3 %copy-start.13 = (bf16[2,3072,256]{2,1,0:T(8,128)(2,1)}, bf16[2,3072,256]{2,1,0:T(8,128)(2,1)S(1)}, u32[]{:S(2)}) copy-start(bf16[2,3072,256]{2,1,0:T(8,128)(2,1)S(1)} %get-tuple-element.32) | copy-start | bytes 9437188
  191.0 4.3 %copy-start.7 = (f32[2,3072,64]{2,1,0:T(8,128)S(1)}, f32[2,3072,64]{2,1,0:T(8,128)}, u32[]{:S(2)}) copy-start(f32[2,3072,64]{2,1,0:T(8,128)} %fusion.51) | copy-start | bytes 4718596
  196.7 12.9 %copy-start.6 = (bf16[2,64,48,128]{3,2,1,0:T(8,128)(2,1)S(1)}, bf16[2,64,48,128]{3,2,1,0:T(8,128)(2,1)}, u32[]{:S(2)}) copy-start(bf16[2,64,48,128]{3,2,1,0:T(8,128)(2,1)} %copy-done.4) | copy-start | bytes 4718596
  204.0 85.8 %all-to-all-start.3 = ((f32[2,1536,128]{2,0,1:T(2,128)}), f32[2,1536,128]{2,0,1:T(2,128)S(1)}, u32[]{:S(2)}, u32[]{:S(2)}) async-start(f32[2,1536,128]{2,0,1:T(2,128)} %copy.133), calls=%async_computation.3 | async-start | bytes 3145728 | tf_op jit(solution)/shard_map/all_to_all | solution.py:183
  209.6 74.7 %all-reduce.6.cloned.1.call-start = ((), (), s32[]{:S(2)}) async-start(), calls=%async_computation.4 | async-start | bytes 3473408 | tf_op jit(solution)/shard_map/psum | solution.py:187
  209.6 2.8 copy-start.14
  217.6 66.7 %copy-start.9 = (f32[2,848,256]{2,1,0:T(8,128)S(1)}, f32[2,848,256]{2,1,0:T(8,128)}, u32[]{:S(2)}) copy-start(f32[2,848,256]{2,1,0:T(8,128)} %param.20) | copy-start | bytes 5210116
  293.6 17.0 %copy-start.19 = (f32[16,64]{1,0:T(8,128)S(1)}, f32[16,64]{1,0:T(8,128)}, u32[]{:S(2)}) copy-start(f32[16,64]{1,0:T(8,128)} %param.23) | copy-start | bytes 12292
  293.6 17.0 %copy-start.20 = (f32[16,64]{1,0:T(8,128)S(1)}, f32[16,64]{1,0:T(8,128)}, u32[]{:S(2)}) copy-start(f32[16,64]{1,0:T(8,128)} %param.24) | copy-start | bytes 12292
  293.6 16.9 %copy-start.21 = (f32[16,64]{1,0:T(8,128)S(1)}, f32[16,64]{1,0:T(8,128)}, u32[]{:S(2)}) copy-start(f32[16,64]{1,0:T(8,128)} %param.25) | copy-start | bytes 12292
Sparse Core Ops, SparseCore 0:
  224.9 59.3 all-reduce.5
where the time goes:
time: 324 us; the launch traced here: 319 us
  waiting for transfers between devices  107 us (33%)
  local copies, waits for them, and re-layouts  89.5 us (28%)
  matrix products  43.6 us (13%)
  other arithmetic  25.5 us (8%)
  starting transfers between devices  24 us (7%)
  between operations  14.9 us (5%)
  blocking collectives  14.1 us (4%)
    psum x1, waiting for transfers between devices, shards(): param_grad = lax.psum(local_grad, 'dp')  58.9 us
    all_to_all x1, waiting for transfers between devices, shards(): lax.all_to_all(outgoing, 'expert', split_axis=0, concat_axis=1, tiled=True)  38.8 us
    gather x3, local copies, waits for them, and re-layouts, pick_rows(): return jnp.take(buffer, slot_index, axis=0, mode='fill', fill_value=0)  30.4 us
    unnamed x64, local copies, waits for them, and re-layouts  17.9 us
    all_to_all x1, blocking collectives, shards(): lax.all_to_all(cot_slots, 'expert', split_axis=0, concat_axis=1, tiled=True)  14.1 us
    scatter x1, other arithmetic, place_rows(): return blank.at[slot_index].set(rows, mode='drop')  13.5 us
    all_to_all x1, starting transfers between devices, shards(): lax.all_to_all(outgoing, 'expert', split_axis=0, concat_axis=1, tiled=True)  12.7 us
    dot_general x4, matrix products, hidden_grads(): jnp.einsum('enr,enw->erw', activations[layer_index], pre_grad, preferred_...  12.6 us
  transfers between devices with their start and end apart: 4, of which 3 were waited for; matrix products, arithmetic and copies ran while one was open for 7% of the time, Pallas kernels for 0%

commit v1 on v0

v1 whole, which is shorter than its diff:
```python
import jax
import jax.numpy as jnp
from jax import lax
from jax.experimental import pallas as pl
from jax.experimental.pallas import tpu as pltpu
from jax.sharding import PartitionSpec as P

NET_WIDTH = 256
CODE_WIDTH = 64
ENC_WIDTH = 64
LAYERS = 4
SAMPLES = 32
RAYS = 128
IMAGES_DEV = 16
CAPACITY = 48
DEPTH = 16
THIRDS = CAPACITY // DEPTH
HEAD_ROW = ENC_WIDTH + (LAYERS - 1) * NET_WIDTH
PARAM_ROWS = HEAD_ROW + 16

F32 = jnp.float32
BF16 = jnp.bfloat16

BETA_ONE = 0.9
BETA_TWO = 0.999
LEARN_RATE = 0.001
ADAM_EPS = 1e-08
CORRECT_ONE = 1.0 - 0.9**10
CORRECT_TWO = 1.0 - 0.999**10

NN = (((1,), (0,)), ((), ()))
NT = (((1,), (1,)), ((), ()))
TN = (((0,), (0,)), ((), ()))


def mul(left, right, dims=NN):
    return lax.dot_general(left, right, dims, preferred_element_type=F32)


def iota(shape, dim):
    return lax.broadcasted_iota(jnp.int32, shape, dim)


def three_parts(value):
    high = value.astype(BF16)
    rest = value - high.astype(F32)
    middle = rest.astype(BF16)
    low = (rest - middle.astype(F32)).astype(BF16)
    return [high, middle, low]


def adam_update(param_now, gradient, moment_one, moment_two):
    new_one = BETA_ONE * moment_one + (1.0 - BETA_ONE) * gradient
    new_two = BETA_TWO * moment_two + (1.0 - BETA_TWO) * gradient * gradient
    update = LEARN_RATE * (new_one / CORRECT_ONE) / (jnp.sqrt(new_two / CORRECT_TWO) + ADAM_EPS)
    return (param_now - update, new_one, new_two)


def dispatch_kernel(feat_ref, cell_ref, rank_ref, out_ref, hot_ref, rows_ref):
    places = out_ref.shape[0]
    for i in range(SAMPLES):
        cell = cell_ref[i : i + 1, :]
        rank = rank_ref[i : i + 1, :]
        place = jnp.where(rank >= 0, (cell >> 1) * DEPTH + (rank & (DEPTH - 1)), -1)
        inner = (rank >> 4) * 2 + (cell & 1)
        span = pl.ds(i * RAYS, RAYS)
        hot_ref[:, span] = jnp.where(iota((places, RAYS), 0) == place, 1.0, 0.0).astype(BF16)
        feat = feat_ref[i].astype(F32)
        for q in range(THIRDS * 2):
            rows_ref[q * ENC_WIDTH : (q + 1) * ENC_WIDTH, span] = jnp.where(
                inner == q, feat, 0.0
            ).astype(BF16)
    out_ref[...] = mul(hot_ref[...], rows_ref[...], NT).astype(BF16)


def depth_match(rows):
    return (iota((rows, 128), 0) & (DEPTH - 1)) == (iota((rows, 128), 1) & (DEPTH - 1))


def first_matrix(weights_ref, held):
    matrix = weights_ref[held, 0:ENC_WIDTH, :]
    blank = jnp.zeros_like(matrix)
    return jnp.concatenate([matrix, blank] if held == 0 else [blank, matrix], axis=0)


def hidden_matrix(weights_ref, held, layer):
    start = ENC_WIDTH + (layer - 1) * NET_WIDTH
    return weights_ref[held, start : start + NET_WIDTH, :]


def head_tile(head, held):
    rows = jnp.concatenate(
        [jnp.broadcast_to(head[c : c + 1, :], (DEPTH, NET_WIDTH)) for c in range(4)], axis=0
    )
    blank = jnp.zeros_like(rows)
    return jnp.concatenate([rows, blank] if held == 0 else [blank, rows], axis=0).astype(BF16)


def forward_kernel(x_ref, params_ref, acts_ref, out_ref, weights_ref):
    third = pl.program_id(0)
    groups = out_ref.shape[0]
    rows = x_ref.shape[0]

    @pl.when(third == 0)
    def _():
        weights_ref[...] = params_ref[...].astype(BF16)

    heads = [weights_ref[h, HEAD_ROW:PARAM_ROWS, :].astype(F32) for h in range(2)]

    @pl.when(third == 0)
    def _():
        for j in range(4):
            h, c = j // 2, (j % 2) * 2
            pair = jnp.concatenate(
                [heads[h][4 + c : 5 + c, :CODE_WIDTH], heads[h][5 + c : 6 + c, :CODE_WIDTH]], axis=1
            )
            out_ref[:, 3 + j, :] = jnp.broadcast_to(pair, (groups, 128))
        out_ref[:, 7, :] = jnp.zeros((groups, 128), F32)

    lane = iota((1, 128), 1)
    shift = jnp.zeros((1, 128), F32)
    total = jnp.zeros((rows, 128), F32)
    for h in range(2):
        current = x_ref[...]
        for k in range(LAYERS):
            matrix = first_matrix(weights_ref, h) if k == 0 else hidden_matrix(weights_ref, h, k)
            preact = mul(current, matrix) + heads[h][9 + k : 10 + k, :]
            current = jnp.maximum(preact, 0.0).astype(BF16)
            acts_ref[0, h, k] = current
        total = total + mul(current, head_tile(heads[h], h), NT)
        for c in range(4):
            shift = shift + jnp.where((lane >> 4) == h * 4 + c, heads[h][8:9, c : c + 1], 0.0)
    total = jnp.where(depth_match(rows), total + shift, 0.0)
    raw = jnp.sum(total.reshape(groups, DEPTH, 128), axis=1)
    for j in range(THIRDS):

        @pl.when(third == j)
        def _():
            out_ref[:, j, :] = raw


def one_sample_row(cell_ref, rank_ref, image, i, owners):
    cell = cell_ref[pl.ds(i, 1), :]
    rank = rank_ref[pl.ds(i, 1), :]
    live = rank >= 0
    owner = jnp.where(live, cell >> 1, -1)
    hot = jnp.where(iota((owners, RAYS), 0) == owner, 1.0, 0.0).astype(BF16)
    held = cell & 1
    slot = jnp.where(live, ((rank >> 4) * 2 + held) * DEPTH + (rank & (DEPTH - 1)), -1)
    code = jnp.where(live, held * IMAGES_DEV + image, -1)
    slot_mask = iota((THIRDS * 2 * DEPTH, RAYS), 0) == slot
    code_mask = iota((2 * IMAGES_DEV, RAYS), 0) == code
    masks = [slot_mask[q * DEPTH : (q + 1) * DEPTH] for q in range(THIRDS * 2)]
    masks += [code_mask[h * IMAGES_DEV : (h + 1) * IMAGES_DEV] for h in range(2)]
    return hot, masks


def running_sum(value):
    step = 1
    while step < SAMPLES:
        value = value + jnp.concatenate(
            [jnp.zeros((step, RAYS), F32), value[: SAMPLES - step]], axis=0
        )
        step *= 2
    return value


def running_sum_back(value):
    step = 1
    while step < SAMPLES:
        value = value + jnp.concatenate([value[step:], jnp.zeros((step, RAYS), F32)], axis=0)
        step *= 2
    return value


def ray_kernel(
    back_ref,
    cell_ref,
    rank_ref,
    image_ref,
    length_ref,
    spacing_ref,
    targets_ref,
    code_ref,
    first_ref,
    second_ref,
    out_ref,
    loss_ref,
    new_code_ref,
    new_first_ref,
    new_second_ref,
    table_ref,
    raw_ref,
):
    owners = back_ref.shape[0]
    image = image_ref[...] & (IMAGES_DEV - 1)
    code = code_ref[...].astype(BF16).astype(F32)
    tile = jnp.concatenate([code] * 8, axis=0)
    tile = jnp.concatenate([tile, tile], axis=1)
    block_row = iota((128, 128), 0) >> 4
    block_lane = iota((128, 128), 1) >> 6
    code_blocks = [
        jnp.where(block_row == 2 * j + block_lane, tile, 0.0).astype(BF16) for j in range(4)
    ]
    queries = [back_ref[:, 3 + j, :].astype(BF16) for j in range(4)]
    code_part = mul(queries[0], code_blocks[0], NT)
    for j in range(1, 4):
        code_part = code_part + mul(queries[j], code_blocks[j], NT)
    pieces = [back_ref[:, j, :] for j in range(THIRDS)] + [code_part]
    table = jnp.concatenate([piece.T for piece in pieces], axis=0)
    table_ref[...] = jnp.concatenate(three_parts(table), axis=1)

    def pick(i, carry):
        hot, masks = one_sample_row(cell_ref, rank_ref, image, i, owners)
        found = mul(table_ref[...], jnp.concatenate([hot] * 3, axis=0))
        for c in range(4):
            total = jnp.zeros((DEPTH, RAYS), F32)
            for q in range(THIRDS * 2 + 2):
                start = q * 64 + c * DEPTH
                total = total + jnp.where(masks[q], found[start : start + DEPTH], 0.0)
            raw_ref[c, pl.ds(i, 1), :] = jnp.sum(total, axis=0, keepdims=True)
        return carry

    lax.fori_loop(0, SAMPLES, pick, 0, unroll=4)

    spacing = spacing_ref[...]
    live = jnp.where(iota((SAMPLES, RAYS), 0) < length_ref[...], 1.0, 0.0)
    raw_density = raw_ref[0]
    small = jnp.exp(-jnp.abs(raw_density))
    density = jnp.maximum(raw_density, 0.0) + jnp.log1p(small)
    slope = jnp.where(raw_density >= 0, 1.0, small) / (1.0 + small)
    colors = []
    for c in range(3):
        raw_color = raw_ref[1 + c]
        tail = jnp.exp(-jnp.abs(raw_color))
        colors.append(jnp.where(raw_color >= 0, 1.0, tail) / (1.0 + tail))
    reach = spacing * live
    tau = density * reach
    before = running_sum(tau) - tau
    passed = jnp.exp(-before)
    kept = jnp.exp(-tau)
    weight = passed * (1.0 - kept)
    gaps = []
    loss = jnp.zeros((1, RAYS), F32)
    for c in range(3):
        gap = jnp.sum(weight * colors[c], axis=0, keepdims=True) - targets_ref[c : c + 1, :]
        gaps.append(gap)
        loss = loss + gap * gap
    loss_ref[...] = 0.5 * loss
    pull = gaps[0] * colors[0] + gaps[1] * colors[1] + gaps[2] * colors[2]
    behind = weight * pull
    tau_grad = pull * passed * kept - (running_sum_back(behind) - behind)
    raw_ref[0] = (tau_grad * reach * slope).astype(BF16).astype(F32)
    for c in range(3):
        raw_ref[1 + c] = (
            (weight * gaps[c] * (colors[c] * (1.0 - colors[c]))).astype(BF16).astype(F32)
        )

    def put(i, total):
        hots, rows = [], []
        for half in range(2):
            hot, masks = one_sample_row(cell_ref, rank_ref, image, 2 * i + half, owners)
            cots = [raw_ref[c, pl.ds(2 * i + half, 1), :] for c in range(4)]
            hots.append(hot)
            rows.append(
                jnp.concatenate(
                    [
                        jnp.where(masks[q], cots[c], 0.0)
                        for q in range(THIRDS * 2 + 2)
                        for c in range(4)
                    ],
                    axis=0,
                ).astype(BF16)
            )
        return total + mul(
            jnp.concatenate(rows, axis=1), jnp.concatenate(hots, axis=1), NT
        )

    placed = lax.fori_loop(
        0, SAMPLES // 2, put, jnp.zeros((512, owners), F32), unroll=2
    )
    for j in range(THIRDS):
        out_ref[:, j, :] = placed[j * 128 : (j + 1) * 128].T
    image_sums = placed[384:512]
    sums_parts = three_parts(image_sums)
    sums_wide = jnp.concatenate(sums_parts, axis=1)
    sums_flip = jnp.concatenate(three_parts(image_sums.T), axis=1)
    table_grad = jnp.zeros((IMAGES_DEV, CODE_WIDTH), F32)
    for j in range(4):
        out_ref[:, 3 + j, :] = mul(sums_flip, jnp.concatenate([code_blocks[j]] * 3, axis=0))
        product = mul(sums_wide, jnp.concatenate([queries[j]] * 3, axis=0))
        low = 2 * j * IMAGES_DEV
        table_grad = table_grad + product[low : low + IMAGES_DEV, :CODE_WIDTH]
        table_grad = table_grad + product[low + IMAGES_DEV : low + 2 * IMAGES_DEV, CODE_WIDTH:]
    out_ref[:, 7, :] = jnp.zeros((owners, 128), F32)
    new_code, new_first, new_second = adam_update(
        code_ref[...], table_grad, first_ref[...], second_ref[...]
    )
    new_code_ref[...] = new_code
    new_first_ref[...] = new_first
    new_second_ref[...] = new_second


def backward_kernel(x_ref, acts_ref, cot_ref, params_ref, grad_ref, weights_ref, total_ref):
    third = pl.program_id(0)
    groups = cot_ref.shape[0]
    rows = x_ref.shape[0]

    @pl.when(third == 0)
    def _():
        weights_ref[...] = params_ref[...].astype(BF16)
        total_ref[...] = jnp.zeros_like(total_ref)
        for h in range(2):
            lines = []
            for c in range(4):
                sums = jnp.sum(cot_ref[:, 3 + h * 2 + c // 2, :], axis=0, keepdims=True)
                start = (c % 2) * CODE_WIDTH
                line = sums[:, start : start + CODE_WIDTH]
                lines.append(
                    jnp.concatenate([line, jnp.zeros((1, NET_WIDTH - CODE_WIDTH), F32)], axis=1)
                )
            total_ref[h, HEAD_ROW:PARAM_ROWS, :] = jnp.concatenate(
                [jnp.zeros((4, NET_WIDTH), F32)] + lines + [jnp.zeros((8, NET_WIDTH), F32)], axis=0
            )

    cot = jnp.where(
        third == 0, cot_ref[:, 0, :], jnp.where(third == 1, cot_ref[:, 1, :], cot_ref[:, 2, :])
    )
    sums = jnp.sum(cot, axis=0, keepdims=True)
    spread = jnp.broadcast_to(cot[:, None, :], (groups, DEPTH, 128)).reshape(rows, 128)
    spread = jnp.where(depth_match(rows), spread, 0.0).astype(BF16)
    lane = iota((1, 128), 1)
    wide_lane = iota((1, NET_WIDTH), 1)
    for h in range(2):
        head = weights_ref[h, HEAD_ROW:PARAM_ROWS, :].astype(F32)
        last = acts_ref[0, h, LAYERS - 1]
        outer = mul(spread, last, TN)[h * 64 : (h + 1) * 64]
        head_grad = jnp.sum(outer.reshape(4, DEPTH, NET_WIDTH), axis=1)
        bias_head = jnp.zeros((1, NET_WIDTH), F32)
        for c in range(4):
            value = jnp.sum(
                jnp.where((lane >> 4) == h * 4 + c, sums, 0.0), axis=1, keepdims=True
            )
            bias_head = bias_head + jnp.where(wide_lane == c, value, 0.0)
        up = mul(spread, head_tile(head, h))
        bias_lines = [None] * LAYERS
        for k in reversed(range(LAYERS)):
            pre_grad = jnp.where(acts_ref[0, h, k].astype(F32) > 0, up, 0.0).astype(BF16)
            bias_lines[k] = jnp.sum(pre_grad.astype(F32), axis=0, keepdims=True)
            if k > 0:
                start = ENC_WIDTH + (k - 1) * NET_WIDTH
                total_ref[h, start : start + NET_WIDTH, :] += mul(
                    acts_ref[0, h, k - 1], pre_grad, TN
                )
                up = mul(pre_grad, hidden_matrix(weights_ref, h, k), NT)
            else:
                total_ref[h, 0:ENC_WIDTH, :] += mul(x_ref[...], pre_grad, TN)[
                    h * ENC_WIDTH : (h + 1) * ENC_WIDTH
                ]
        total_ref[h, HEAD_ROW:PARAM_ROWS, :] += jnp.concatenate(
            [head_grad, jnp.zeros((4, NET_WIDTH), F32), bias_head]
            + bias_lines
            + [jnp.zeros((3, NET_WIDTH), F32)],
            axis=0,
        )

    @pl.when(third == THIRDS - 1)
    def _():
        grad_ref[...] = total_ref[...].astype(BF16)


def limits(mib=48):
    return pltpu.CompilerParams(vmem_limit_bytes=mib * 1024 * 1024)


def shape_of(dims, kind):
    return jax.ShapeDtypeStruct(dims, kind)


def shards(
    features,
    spacing,
    targets,
    ray_length,
    cell_id,
    slot_rank,
    image_id,
    params,
    first_moment,
    second_moment,
    code_table,
    table_first,
    table_second,
):
    groups = lax.axis_size("expert")
    copies = lax.axis_size("dp")
    places = groups * DEPTH
    cell_rows = cell_id.T
    rank_rows = slot_rank.T
    outgoing = pl.pallas_call(
        dispatch_kernel,
        out_shape=shape_of((places, THIRDS * 128), BF16),
        scratch_shapes=[
            pltpu.VMEM((places, SAMPLES * RAYS), BF16),
            pltpu.VMEM((THIRDS * 128, SAMPLES * RAYS), BF16),
        ],
        compiler_params=limits(),
        name="dispatch",
    )(jnp.transpose(features, (1, 2, 0)), cell_rows, rank_rows)
    arrived = lax.all_to_all(outgoing, "expert", split_axis=0, concat_axis=0, tiled=True)

    whole = lambda *dims: pl.BlockSpec(dims, lambda i: (0,) * len(dims))
    third_rows = pl.BlockSpec((places, 128), lambda i: (0, i))
    third_acts = pl.BlockSpec((1, 2, LAYERS, places, NET_WIDTH), lambda i: (i, 0, 0, 0, 0))
    acts, raw_out = pl.pallas_call(
        forward_kernel,
        grid=(THIRDS,),
        in_specs=[third_rows, whole(2, PARAM_ROWS, NET_WIDTH)],
        out_specs=[third_acts, whole(groups, 8, 128)],
        out_shape=[
            shape_of((THIRDS, 2, LAYERS, places, NET_WIDTH), BF16),
            shape_of((groups, 8, 128), F32),
        ],
        scratch_shapes=[pltpu.VMEM((2, PARAM_ROWS, NET_WIDTH), BF16)],
        compiler_params=limits(),
        name="forward",
    )(arrived, params)
    returned = lax.all_to_all(raw_out, "expert", split_axis=0, concat_axis=0, tiled=True)

    table_shape = shape_of(code_table.shape, F32)
    cot_out, loss, new_table, new_table_first, new_table_second = pl.pallas_call(
        ray_kernel,
        out_shape=[
            shape_of((groups, 8, 128), F32),
            shape_of((1, RAYS), F32),
            table_shape,
            table_shape,
            table_shape,
        ],
        scratch_shapes=[
            pltpu.VMEM((512, 3 * groups), BF16),
            pltpu.VMEM((4, SAMPLES, RAYS), F32),
        ],
        compiler_params=limits(),
        name="rays",
    )(
        returned,
        cell_rows,
        rank_rows,
        image_id.reshape(1, RAYS),
        ray_length.reshape(1, RAYS),
        spacing.T,
        targets,
        code_table,
        table_first,
        table_second,
    )
    cot_in = lax.all_to_all(cot_out, "expert", split_axis=0, concat_axis=0, tiled=True)

    local_grad = pl.pallas_call(
        backward_kernel,
        grid=(THIRDS,),
        in_specs=[
            third_rows,
            third_acts,
            whole(groups, 8, 128),
            whole(2, PARAM_ROWS, NET_WIDTH),
        ],
        out_specs=whole(2, PARAM_ROWS, NET_WIDTH),
        out_shape=shape_of((2, PARAM_ROWS, NET_WIDTH), BF16),
        scratch_shapes=[
            pltpu.VMEM((2, PARAM_ROWS, NET_WIDTH), BF16),
            pltpu.VMEM((2, PARAM_ROWS, NET_WIDTH), F32),
        ],
        compiler_params=limits(),
        name="backward",
    )(arrived, acts, cot_in, params)

    quarter = 2 * PARAM_ROWS // copies
    shares = lax.all_to_all(
        local_grad.reshape(copies, quarter, NET_WIDTH), "dp", split_axis=0, concat_axis=0, tiled=True
    )
    share = jnp.sum(shares.astype(F32), axis=0).astype(BF16)
    param_grad = (
        lax.all_gather(share, "dp", axis=0, tiled=False)
        .reshape(2, PARAM_ROWS, NET_WIDTH)
        .astype(F32)
    )
    new_params, new_first, new_second = adam_update(params, param_grad, first_moment, second_moment)
    return (
        loss.reshape(RAYS),
        new_params,
        new_first,
        new_second,
        new_table,
        new_table_first,
        new_table_second,
    )


def solution(mesh):
    rays = ("expert", "dp")
    table = P(rays, None)
    block = P("expert", None, None)
    return jax.shard_map(
        shards,
        mesh=mesh,
        in_specs=(
            P(rays, None, None),
            P(rays, None),
            P(None, rays),
            P(rays),
            P(rays, None),
            P(rays, None),
            P(rays),
            block,
            block,
            block,
            table,
            table,
            table,
        ),
        out_specs=(P(rays), block, block, block, table, table, table),
        check_vma=False,
    )
```

time: 324 us -> 143 us (0.44); the launches traced: 319 us -> 143 us
  waiting for transfers between devices: 107 us -> 0 us
  blocking collectives: 14.1 us -> 103 us
  local copies, waits for them, and re-layouts: 89.5 us -> 2.65 us
  matrix products: 43.6 us -> 0 us
  Pallas kernels: 0 us -> 31.5 us
  starting transfers between devices: 24 us -> 0 us
  other arithmetic: 25.5 us -> 5.19 us
  between operations: 14.9 us -> 0.77 us
    all_to_all x1 -> x4, blocking collectives: 14.1 us -> 88.2 us  [the longest x1 35 us: shards(): lax.all_to_all(outgoing, 'expert', split_axis=0, concat_axis=0, tiled=True)]
    psum x1 -> x0, waiting for transfers between devices: 58.9 us -> none  [shards(): param_grad = lax.psum(local_grad, 'dp')]
    all_to_all x3 -> x0, waiting for transfers between devices: 48.1 us -> none  [the longest x1 38.8 us: shards(): lax.all_to_all(outgoing, 'expert', split_axis=0, concat_axis=1, tiled=True)]
    dot_general x19 -> x0, matrix products: 43.6 us -> none  [the longest x4 12.6 us: hidden_grads(): jnp.einsum('enr,enw->erw', activations[layer_index], pre_grad, preferred_...]
    pallas_call x0 -> x4, Pallas kernels: none -> 31.5 us  [the longest x1 11.3 us: shards(): pl.pallas_call(backward_kernel, grid=(THIRDS,), in_specs=[third_rows, thi...]
    gather x3 -> x0, local copies, waits for them, and re-layouts: 30.4 us -> none  [pick_rows(): return jnp.take(buffer, slot_index, axis=0, mode='fill', fill_value=0)]
    all_to_all x3 -> x0, starting transfers between devices: 24 us -> none  [the longest x1 12.7 us: shards(): lax.all_to_all(outgoing, 'expert', split_axis=0, concat_axis=1, tiled=True)]
    unnamed x64 -> x26, local copies, waits for them, and re-layouts: 17.9 us -> 2.65 us
  transfers between devices with their start and end apart: 4 -> 0, of which waited for: 3 -> 0; matrix products, arithmetic and copies ran while one was open for 7% -> 0% of each run, Pallas kernels for 0% -> 0%
where the time goes in v1:
time: 143 us
  blocking collectives  103 us (72%)
  Pallas kernels  31.5 us (22%)
  other arithmetic  5.19 us (4%)
  local copies, waits for them, and re-layouts  2.65 us (2%)
    all_to_all x1, blocking collectives, shards(): lax.all_to_all(outgoing, 'expert', split_axis=0, concat_axis=0, tiled=True)  35 us
    all_to_all x1, blocking collectives, shards(): lax.all_to_all(raw_out, 'expert', split_axis=0, concat_axis=0, tiled=True)  17.8 us
    all_to_all x1, blocking collectives, shards(): lax.all_to_all(local_grad.reshape(copies, quarter, NET_WIDTH), 'dp', spli...  17.7 us
    all_to_all x1, blocking collectives, shards(): lax.all_to_all(cot_out, 'expert', split_axis=0, concat_axis=0, tiled=True)  17.7 us
    all_gather x1, blocking collectives, shards(): lax.all_gather(share, 'dp', axis=0, tiled=False)  14.5 us
    pallas_call x1, Pallas kernels, shards(): pl.pallas_call(backward_kernel, grid=(THIRDS,), in_specs=[third_rows, thi...  11.3 us
    pallas_call x1, Pallas kernels, shards(): pl.pallas_call(ray_kernel, out_shape=[shape_of((groups, 8, 128), F32), sh...  7.63 us
    pallas_call x1, Pallas kernels, shards(): pl.pallas_call(forward_kernel, grid=(THIRDS,), in_specs=[third_rows, whol...  7.51 us

profile of v1, /device:TPU:2, one launch (start us, length us, event | category | flops | bytes accessed | tf_op | source)
XLA Modules:
  0.0 142.9 jit_solution(12218084807743013076)
XLA Ops:
  0.6 0.0 copy-start
  0.6 0.0 copy-start.1
  0.7 1.2 copy-done.1
  1.8 0.0 copy-start.2
  1.8 0.7 copy-done.2
  2.5 0.0 copy-start.4
  2.5 0.7 copy-done.4
  3.2 5.1 %dispatch.1 = bf16[1024,384]{1,0:T(8,128)(2,1)S(1)} custom-call(bf16[32,64,128]{2,1,0:T(8,128)(2,1)S(1)} %bitcast.16, s32[32,128]{1,0:T(8,128)S(1)} %bitcast.17, s32[32,128]{1,0:T(8,128)S(1)} %bitcast.19), custom_call_target="tpu_custom_call" | custom-call | tf_op jit(solution)/shard_map/dispatch/pallas_call | solution.py:400
  8.4 35.0 %all_to_all.26 = bf16[64,16,384]{2,1,0:T(8,128)(2,1)S(1)} all-to-all(bf16[64,16,384]{2,1,0:T(8,128)(2,1)S(1)} %bitcast.15), channel_id=1, replica_groups=mesh['expert'=64,'dp'=4] {'expert'}, dimensions={0} | all-to-all | bytes 1572864 | tf_op jit(solution)/shard_map/all_to_all | solution.py:410
  43.4 0.0 copy-start.3
  43.4 0.0 copy-start.5
  43.4 0.0 copy-start.6
  43.4 0.0 copy-start.7
  43.4 0.0 copy-start.8
  43.4 0.0 copy-start.9
  43.4 0.0 copy-start.10
  43.4 0.0 copy-start.11
  43.4 0.0 copy-start.12
  43.4 0.0 copy-done
  43.4 7.5 %forward.1 = (bf16[3,2,4,1024,256]{4,3,2,1,0:T(8,128)(2,1)}, f32[64,8,128]{2,1,0:T(8,128)S(1)}) custom-call(bf16[1024,384]{1,0:T(8,128)(2,1)S(1)} %bitcast.12, f32[2,848,256]{2,1,0:T(8,128)S(1)} %copy-done), custom_call_target="tpu_custom_call" | custom-call | tf_op jit(solution)/shard_map/forward/pallas_call | solution.py:415
  51.0 17.8 %all_to_all.27.back_ref = f32[64,8,128]{2,1,0:T(8,128)S(1)} all-to-all(f32[64,8,128]{2,1,0:T(8,128)S(1)} %get-tuple-element.14), channel_id=1, replica_groups=mesh['expert'=64,'dp'=4] {'expert'}, dimensions={0} | all-to-all | bytes 524288 | tf_op jit(solution)/shard_map/all_to_all | solution.py:428
  68.8 0.0 copy-done.3
  68.8 0.0 copy-done.5
  68.8 0.0 copy-done.6
  68.8 0.0 copy-done.7
  68.8 0.0 copy-done.8
  68.8 0.0 copy-done.9
  68.8 0.0 copy-done.10
  68.8 0.0 copy-done.11
  68.8 0.0 copy-done.12
  68.8 7.6 %rays.1 = (f32[64,8,128]{2,1,0:T(8,128)S(1)}, f32[1,128]{1,0:T(1,128)}, f32[16,64]{1,0:T(8,128)}, f32[16,64]{1,0:T(8,128)}, f32[16,64]{1,0:T(8,128)}) custom-call(f32[64,8,128]{2,1,0:T(8,128)S(1)} %all_to_all.27.back_ref, s32[32,128]{1,0:T(8,128)S(1)} %bitcast.18, s32[32,128]{1,0:T(8,128)S(1)} %bitcast.20, s32[1,128]{1,0:T(1,128)S(1)} %bitcast.22, ...), custom_call_target="tpu_custom_call" | custom-call | tf_op jit(solution)/shard_map/rays/pallas_call | solution.py:431
  76.5 17.7 %all_to_all.28.cot_ref = f32[64,8,128]{2,1,0:T(8,128)S(1)} all-to-all(f32[64,8,128]{2,1,0:T(8,128)S(1)} %get-tuple-element.17), channel_id=1, replica_groups=mesh['expert'=64,'dp'=4] {'expert'}, dimensions={0} | all-to-all | bytes 524288 | tf_op jit(solution)/shard_map/all_to_all | solution.py:458
  94.1 11.3 %backward.1 = bf16[2,848,256]{2,1,0:T(8,128)(2,1)S(1)} custom-call(bf16[1024,384]{1,0:T(8,128)(2,1)S(1)} %bitcast.13, bf16[3,2,4,1024,256]{4,3,2,1,0:T(8,128)(2,1)} %get-tuple-element.16.acts_ref, f32[64,8,128]{2,1,0:T(8,128)S(1)} %all_to_all.28.cot_ref, f32[2,848,256]{2,1,0:T(8,128)S(1)} %copy-done), custom_call_target="tpu_custom_call" | custom-call | tf_op jit(solution)/shard_map/backward/pallas_call | solution.py:460
  105.4 17.7 %all_to_all.29 = bf16[4,424,256]{2,1,0:T(8,128)(2,1)S(1)} all-to-all(bf16[4,424,256]{2,1,0:T(8,128)(2,1)S(1)} %bitcast.14), channel_id=1, replica_groups=mesh['expert'=64,'dp'=4] {'dp'}, dimensions={0} | all-to-all | bytes 1736704 | tf_op jit(solution)/shard_map/all_to_all | solution.py:480
  123.2 0.2 reduce_sum.12
  123.4 14.5 %all-gather = bf16[1696,256]{1,0:T(8,128)(2,1)S(1)} all-gather(bf16[424,256]{1,0:T(8,128)(2,1)S(1)} %reduce_sum.12), channel_id=2, replica_groups=mesh['expert'=64,'dp'=4] {'dp'}, dimensions={0}, use_global_device_ids=true | all-gather | bytes 1085440 | tf_op jit(solution)/shard_map/all_gather | solution.py:485
  137.9 5.0 %divide_subtract_fusion = (f32[2,848,256]{2,1,0:T(8,128)}, f32[2,848,256]{2,1,0:T(8,128)}, f32[2,848,256]{2,1,0:T(8,128)}) fusion(f32[2,848,256]{2,1,0:T(8,128)S(1)} %copy-done, bf16[2,848,256]{2,1,0:T(8,128)(2,1)S(1)} %bitcast.24, f32[2,848,256]{2,1,0:T(8,128)} %param.21, f32[2,848,256]{2,1,0:T(8,128)} %param.22), kind=kLoop, calls=%fused_computation.5 | loop fusion | flops 5644288 | bytes 11288576 | tf_op jit(solution)/shard_map/sub | solution.py:56
Async XLA Ops:
  0.6 42.8 %copy-start = (f32[2,848,256]{2,1,0:T(8,128)S(1)}, f32[2,848,256]{2,1,0:T(8,128)}, u32[]{:S(2)}) copy-start(f32[2,848,256]{2,1,0:T(8,128)} %params_ref.3) | copy-start | bytes 5210116
  0.6 1.2 copy-start.1
  1.8 0.7 copy-start.2
  2.5 0.7 copy-start.4
  43.4 25.4 %copy-start.3 = (s32[128,32]{0,1:T(8,128)S(1)}, s32[128,32]{0,1:T(8,128)}, u32[]{:S(2)}) copy-start(s32[128,32]{0,1:T(8,128)} %param.17) | copy-start | bytes 49156
  43.4 25.4 %copy-start.5 = (s32[128,32]{0,1:T(8,128)S(1)}, s32[128,32]{0,1:T(8,128)}, u32[]{:S(2)}) copy-start(s32[128,32]{0,1:T(8,128)} %param.18) | copy-start | bytes 49156
  43.4 25.4 %copy-start.6 = (f32[128,32]{0,1:T(8,128)S(1)}, f32[128,32]{0,1:T(8,128)}, u32[]{:S(2)}) copy-start(f32[128,32]{0,1:T(8,128)} %param.14) | copy-start | bytes 49156
  43.4 25.4 %copy-start.7 = (f32[16,64]{1,0:T(8,128)S(1)}, f32[16,64]{1,0:T(8,128)}, u32[]{:S(2)}) copy-start(f32[16,64]{1,0:T(8,128)} %code_ref.1) | copy-start | bytes 12292
  43.4 25.4 %copy-start.8 = (f32[16,64]{1,0:T(8,128)S(1)}, f32[16,64]{1,0:T(8,128)}, u32[]{:S(2)}) copy-start(f32[16,64]{1,0:T(8,128)} %first_ref.1) | copy-start | bytes 12292
  43.4 25.4 %copy-start.9 = (f32[16,64]{1,0:T(8,128)S(1)}, f32[16,64]{1,0:T(8,128)}, u32[]{:S(2)}) copy-start(f32[16,64]{1,0:T(8,128)} %second_ref.1) | copy-start | bytes 12292
  43.4 25.4 %copy-start.10 = (f32[3,128]{1,0:T(4,128)S(1)}, f32[3,128]{1,0:T(4,128)}, u32[]{:S(2)}) copy-start(f32[3,128]{1,0:T(4,128)} %targets_ref.1) | copy-start | bytes 4612
  43.4 25.4 %copy-start.11 = (s32[128]{0:T(128)S(1)}, s32[128]{0:T(128)}, u32[]{:S(2)}) copy-start(s32[128]{0:T(128)} %param.19) | copy-start | bytes 1540
  43.4 25.4 %copy-start.12 = (s32[128]{0:T(128)S(1)}, s32[128]{0:T(128)}, u32[]{:S(2)}) copy-start(s32[128]{0:T(128)} %param.16) | copy-start | bytes 1540

commit v2 on v1

--- a/solution.py
+++ b/solution.py
@@ -191,6 +191,7 @@
     new_second_ref,
     table_ref,
     raw_ref,
+    lines_ref,
 ):
     owners = back_ref.shape[0]
     image = image_ref[...] & (IMAGES_DEV - 1)
@@ -280,19 +281,20 @@
         0, SAMPLES // 2, put, jnp.zeros((512, owners), F32), unroll=2
     )
     for j in range(THIRDS):
-        out_ref[:, j, :] = placed[j * 128 : (j + 1) * 128].T
+        lines_ref[:, j, :] = placed[j * 128 : (j + 1) * 128].T
     image_sums = placed[384:512]
     sums_parts = three_parts(image_sums)
     sums_wide = jnp.concatenate(sums_parts, axis=1)
     sums_flip = jnp.concatenate(three_parts(image_sums.T), axis=1)
     table_grad = jnp.zeros((IMAGES_DEV, CODE_WIDTH), F32)
     for j in range(4):
-        out_ref[:, 3 + j, :] = mul(sums_flip, jnp.concatenate([code_blocks[j]] * 3, axis=0))
+        lines_ref[:, 3 + j, :] = mul(sums_flip, jnp.concatenate([code_blocks[j]] * 3, axis=0))
         product = mul(sums_wide, jnp.concatenate([queries[j]] * 3, axis=0))
         low = 2 * j * IMAGES_DEV
         table_grad = table_grad + product[low : low + IMAGES_DEV, :CODE_WIDTH]
         table_grad = table_grad + product[low + IMAGES_DEV : low + 2 * IMAGES_DEV, CODE_WIDTH:]
-    out_ref[:, 7, :] = jnp.zeros((owners, 128), F32)
+    lines_ref[:, 7, :] = jnp.zeros((owners, 128), F32)
+    out_ref[...] = lines_ref[...].astype(BF16)
     new_code, new_first, new_second = adam_update(
         code_ref[...], table_grad, first_ref[...], second_ref[...]
     )
@@ -301,7 +303,20 @@
     new_second_ref[...] = new_second
 
 
-def backward_kernel(x_ref, acts_ref, cot_ref, params_ref, grad_ref, weights_ref, total_ref):
+def backward_kernel(
+    order_ref,
+    x_ref,
+    acts_ref,
+    cot_in_ref,
+    params_ref,
+    own_ref,
+    first_ref,
+    second_ref,
+    third_ref,
+    weights_ref,
+    total_ref,
+    cot_ref,
+):
     third = pl.program_id(0)
     groups = cot_ref.shape[0]
     rows = x_ref.shape[0]
@@ -309,6 +324,7 @@
     @pl.when(third == 0)
     def _():
         weights_ref[...] = params_ref[...].astype(BF16)
+        cot_ref[...] = cot_in_ref[...].astype(F32)
         total_ref[...] = jnp.zeros_like(total_ref)
         for h in range(2):
             lines = []
@@ -319,7 +335,7 @@
                 lines.append(
                     jnp.concatenate([line, jnp.zeros((1, NET_WIDTH - CODE_WIDTH), F32)], axis=1)
                 )
-            total_ref[h, HEAD_ROW:PARAM_ROWS, :] = jnp.concatenate(
+            total_ref[h * PARAM_ROWS + HEAD_ROW : (h + 1) * PARAM_ROWS, :] = jnp.concatenate(
                 [jnp.zeros((4, NET_WIDTH), F32)] + lines + [jnp.zeros((8, NET_WIDTH), F32)], axis=0
             )
 
@@ -348,16 +364,17 @@
             pre_grad = jnp.where(acts_ref[0, h, k].astype(F32) > 0, up, 0.0).astype(BF16)
             bias_lines[k] = jnp.sum(pre_grad.astype(F32), axis=0, keepdims=True)
             if k > 0:
-                start = ENC_WIDTH + (k - 1) * NET_WIDTH
-                total_ref[h, start : start + NET_WIDTH, :] += mul(
+                start = h * PARAM_ROWS + ENC_WIDTH + (k - 1) * NET_WIDTH
+                total_ref[start : start + NET_WIDTH, :] += mul(
                     acts_ref[0, h, k - 1], pre_grad, TN
                 )
                 up = mul(pre_grad, hidden_matrix(weights_ref, h, k), NT)
             else:
-                total_ref[h, 0:ENC_WIDTH, :] += mul(x_ref[...], pre_grad, TN)[
+                start = h * PARAM_ROWS
+                total_ref[start : start + ENC_WIDTH, :] += mul(x_ref[...], pre_grad, TN)[
                     h * ENC_WIDTH : (h + 1) * ENC_WIDTH
                 ]
-        total_ref[h, HEAD_ROW:PARAM_ROWS, :] += jnp.concatenate(
+        total_ref[h * PARAM_ROWS + HEAD_ROW : (h + 1) * PARAM_ROWS, :] += jnp.concatenate(
             [head_grad, jnp.zeros((4, NET_WIDTH), F32), bias_head]
             + bias_lines
             + [jnp.zeros((3, NET_WIDTH), F32)],
@@ -366,7 +383,27 @@
 
     @pl.when(third == THIRDS - 1)
     def _():
-        grad_ref[...] = total_ref[...].astype(BF16)
+        quarter = own_ref.shape[0]
+        for k, share_ref in enumerate((own_ref, first_ref, second_ref, third_ref)):
+            start = pl.multiple_of(order_ref[k] * quarter, 8)
+            share_ref[...] = total_ref[pl.ds(start, quarter), :].astype(share_ref.dtype)
+
+
+def adam_kernel(
+    order_ref, own_ref, first_ref, second_ref, third_ref, *refs
+):
+    step = pl.program_id(0)
+    param_ref, one_ref, two_ref, new_param_ref, new_one_ref, new_two_ref = refs
+    for k, share_ref in enumerate((own_ref, first_ref, second_ref, third_ref)):
+
+        @pl.when(step == k)
+        def _():
+            new_param, new_one, new_two = adam_update(
+                param_ref[...], share_ref[...].astype(F32), one_ref[...], two_ref[...]
+            )
+            new_param_ref[...] = new_param
+            new_one_ref[...] = new_one
+            new_two_ref[...] = new_two
 
 
 def limits(mib=48):
@@ -393,7 +430,6 @@
     table_second,
 ):
     groups = lax.axis_size("expert")
-    copies = lax.axis_size("dp")
     places = groups * DEPTH
     cell_rows = cell_id.T
     rank_rows = slot_rank.T
@@ -431,7 +467,7 @@
     cot_out, loss, new_table, new_table_first, new_table_second = pl.pallas_call(
         ray_kernel,
         out_shape=[
-            shape_of((groups, 8, 128), F32),
+            shape_of((groups, 8, 128), BF16),
             shape_of((1, RAYS), F32),
             table_shape,
             table_shape,
@@ -440,6 +476,7 @@
         scratch_shapes=[
             pltpu.VMEM((512, 3 * groups), BF16),
             pltpu.VMEM((4, SAMPLES, RAYS), F32),
+            pltpu.VMEM((groups, 8, 128), F32),
         ],
         compiler_params=limits(),
         name="rays",
@@ -457,36 +494,71 @@
     )
     cot_in = lax.all_to_all(cot_out, "expert", split_axis=0, concat_axis=0, tiled=True)
 
-    local_grad = pl.pallas_call(
+    copies = lax.axis_size("dp")
+    quarter = 2 * PARAM_ROWS // copies
+    turns = jnp.arange(copies, dtype=jnp.int32)
+    position = lax.axis_index("dp")
+    lent = lambda *dims: pl.BlockSpec(dims, lambda i, order: (0,) * len(dims))
+    shares = pl.pallas_call(
         backward_kernel,
-        grid=(THIRDS,),
-        in_specs=[
-            third_rows,
-            third_acts,
-            whole(groups, 8, 128),
-            whole(2, PARAM_ROWS, NET_WIDTH),
-        ],
-        out_specs=whole(2, PARAM_ROWS, NET_WIDTH),
-        out_shape=shape_of((2, PARAM_ROWS, NET_WIDTH), BF16),
-        scratch_shapes=[
-            pltpu.VMEM((2, PARAM_ROWS, NET_WIDTH), BF16),
-            pltpu.VMEM((2, PARAM_ROWS, NET_WIDTH), F32),
-        ],
+        grid_spec=pltpu.PrefetchScalarGridSpec(
+            num_scalar_prefetch=1,
+            grid=(THIRDS,),
+            in_specs=[
+                pl.BlockSpec((places, 128), lambda i, order: (0, i)),
+                pl.BlockSpec(
+                    (1, 2, LAYERS, places, NET_WIDTH), lambda i, order: (i, 0, 0, 0, 0)
+                ),
+                lent(groups, 8, 128),
+                lent(2, PARAM_ROWS, NET_WIDTH),
+            ],
+            out_specs=[lent(quarter, NET_WIDTH)] * 4,
+            scratch_shapes=[
+                pltpu.VMEM((2, PARAM_ROWS, NET_WIDTH), BF16),
+                pltpu.VMEM((2 * PARAM_ROWS, NET_WIDTH), F32),
+                pltpu.VMEM((groups, 8, 128), F32),
+            ],
+        ),
+        out_shape=[shape_of((quarter, NET_WIDTH), F32)]
+        + [shape_of((quarter, NET_WIDTH), BF16)] * 3,
         compiler_params=limits(),
         name="backward",
-    )(arrived, acts, cot_in, params)
-
-    quarter = 2 * PARAM_ROWS // copies
-    shares = lax.all_to_all(
-        local_grad.reshape(copies, quarter, NET_WIDTH), "dp", split_axis=0, concat_axis=0, tiled=True
-    )
-    share = jnp.sum(shares.astype(F32), axis=0).astype(BF16)
-    param_grad = (
-        lax.all_gather(share, "dp", axis=0, tiled=False)
-        .reshape(2, PARAM_ROWS, NET_WIDTH)
-        .astype(F32)
-    )
-    new_params, new_first, new_second = adam_update(params, param_grad, first_moment, second_moment)
+    )((position + turns) % copies, arrived, acts, cot_in, params)
+
+    def send(value, distance):
+        return lax.ppermute(value, "dp", [(i, (i + distance) % copies) for i in range(copies)])
+
+    share = shares[0]
+    for k in (2, 1, 3):
+        share = share + send(shares[k], k).astype(F32)
+    share = share.astype(BF16)
+    others = [None, None, None]
+    for k in (2, 1, 3):
+        others[k - 1] = send(share, k)
+    flat = (2 * PARAM_ROWS, NET_WIDTH)
+    by_order = pl.BlockSpec((quarter, NET_WIDTH), lambda i, order: (order[i], 0))
+    new_params, new_first, new_second = pl.pallas_call(
+        adam_kernel,
+        grid_spec=pltpu.PrefetchScalarGridSpec(
+            num_scalar_prefetch=1,
+            grid=(copies,),
+            in_specs=[lent(quarter, NET_WIDTH)] * 4 + [by_order] * 3,
+            out_specs=[by_order] * 3,
+        ),
+        out_shape=[shape_of(flat, F32)] * 3,
+        compiler_params=limits(),
+        name="adam",
+    )(
+        (position - turns) % copies,
+        share,
+        *others,
+        params.reshape(flat),
+        first_moment.reshape(flat),
+        second_moment.reshape(flat),
+    )
+    new_params, new_first, new_second = (
+        value.reshape(params.shape) for value in (new_params, new_first, new_second)
+    )
     return (
         loss.reshape(RAYS),
         new_params,

time: 143 us -> 141 us (0.986); the launches traced: 143 us -> 138 us
  blocking collectives: 103 us -> 52.8 us
  waiting for transfers between devices: 0 us -> 29.5 us
  starting transfers between devices: 0 us -> 15.9 us
  other arithmetic: 5.19 us -> 0.14 us
  Pallas kernels: 31.5 us -> 36.3 us
    all_to_all x2 -> x0, blocking collectives: 35.4 us -> none  [the longest x1 17.7 us: shards(): lax.all_to_all(local_grad.reshape(copies, quarter, NET_WIDTH), 'dp', spli...]
    ppermute x0 -> x6, waiting for transfers between devices: none -> 19.6 us  [send(): lax.ppermute(value, 'dp', [(i, (i + distance) % copies) for i in range(co...]
    all_gather x1 -> x0, blocking collectives: 14.5 us -> none  [shards(): lax.all_gather(share, 'dp', axis=0, tiled=False)]
    ppermute x0 -> x6, starting transfers between devices: none -> 10.2 us  [send(): lax.ppermute(value, 'dp', [(i, (i + distance) % copies) for i in range(co...]
    all_to_all x0 -> x1, waiting for transfers between devices: none -> 9.93 us  [shards(): lax.all_to_all(cot_out, 'expert', split_axis=0, concat_axis=0, tiled=True)]
    all_to_all x0 -> x1, starting transfers between devices: none -> 5.66 us  [shards(): lax.all_to_all(cot_out, 'expert', split_axis=0, concat_axis=0, tiled=True)]
    sub x1 -> x0, other arithmetic: 4.99 us -> none  [adam_update(): return (param_now - update, new_one, new_two)]
    pallas_call x2 -> x3, Pallas kernels: 18.9 us -> 23.7 us  [the longest x1 12.2 us: shards(): pl.pallas_call(backward_kernel, grid_spec=pltpu.PrefetchScalarGridSpec(nu...]
  transfers between devices with their start and end apart: 0 -> 7, of which waited for: 0 -> 7; matrix products, arithmetic and copies ran while one was open for 0% -> 0% of each run, Pallas kernels for 0% -> 0%
where the time goes in v2:
time: 141 us; the launch traced here: 138 us
  blocking collectives  52.8 us (37%)
  Pallas kernels  36.3 us (26%)
  waiting for transfers between devices  29.5 us (21%)
  starting transfers between devices  15.9 us (11%)
  local copies, waits for them, and re-layouts  2.65 us (2%)
    all_to_all x1, blocking collectives, shards(): lax.all_to_all(outgoing, 'expert', split_axis=0, concat_axis=0, tiled=True)  35 us
    ppermute x6, waiting for transfers between devices, send(): lax.ppermute(value, 'dp', [(i, (i + distance) % copies) for i in range(co...  19.6 us
    all_to_all x1, blocking collectives, shards(): lax.all_to_all(raw_out, 'expert', split_axis=0, concat_axis=0, tiled=True)  17.8 us
    pallas_call x1, Pallas kernels, shards(): pl.pallas_call(backward_kernel, grid_spec=pltpu.PrefetchScalarGridSpec(nu...  12.2 us
    ppermute x6, starting transfers between devices, send(): lax.ppermute(value, 'dp', [(i, (i + distance) % copies) for i in range(co...  10.2 us
    all_to_all x1, waiting for transfers between devices, shards(): lax.all_to_all(cot_out, 'expert', split_axis=0, concat_axis=0, tiled=True)  9.93 us
    pallas_call x1, Pallas kernels, shards(): pl.pallas_call(ray_kernel, out_shape=[shape_of((groups, 8, 128), BF16), s...  7.71 us
    pallas_call x1, Pallas kernels, shards(): pl.pallas_call(forward_kernel, grid=(THIRDS,), in_specs=[third_rows, whol...  7.51 us
  transfers between devices with their start and end apart: 7, of which 7 were waited for; matrix products, arithmetic and copies ran while one was open for 0% of the time, Pallas kernels for 0%

profile of v2, /device:TPU:2, one launch (start us, length us, event | category | flops | bytes accessed | tf_op | source)
XLA Modules:
  0.0 138.1 jit_solution(11887113522719535871)
XLA Ops:
  0.6 0.0 copy-start
  0.6 0.0 copy-start.3
  0.7 1.2 copy-done.3
  1.8 0.0 copy-start.4
  1.8 0.7 copy-done.4
  2.5 0.0 copy-start.6
  2.5 0.7 copy-done.6
  3.2 5.1 %dispatch.1 = bf16[1024,384]{1,0:T(8,128)(2,1)S(1)} custom-call(bf16[32,64,128]{2,1,0:T(8,128)(2,1)S(1)} %bitcast.21, s32[32,128]{1,0:T(8,128)S(1)} %bitcast.22, s32[32,128]{1,0:T(8,128)S(1)} %bitcast.24), custom_call_target="tpu_custom_call" | custom-call | tf_op jit(solution)/shard_map/dispatch/pallas_call | solution.py:436
  8.4 35.0 %all_to_all.21 = bf16[64,16,384]{2,1,0:T(8,128)(2,1)S(1)} all-to-all(bf16[64,16,384]{2,1,0:T(8,128)(2,1)S(1)} %bitcast.18), channel_id=1, replica_groups=mesh['expert'=64,'dp'=4] {'expert'}, dimensions={0} | all-to-all | bytes 1572864 | tf_op jit(solution)/shard_map/all_to_all | solution.py:446
  43.4 0.0 copy-start.5
  43.4 0.0 copy-start.7
  43.4 0.0 copy-start.10
  43.4 0.0 copy-start.11
  43.4 0.0 copy-start.12
  43.4 0.0 copy-start.13
  43.4 0.0 copy-start.14
  43.4 0.0 copy-done
  43.4 7.5 %forward.1 = (bf16[3,2,4,1024,256]{4,3,2,1,0:T(8,128)(2,1)}, f32[64,8,128]{2,1,0:T(8,128)S(1)}) custom-call(bf16[1024,384]{1,0:T(8,128)(2,1)S(1)} %bitcast.16, f32[2,848,256]{2,1,0:T(8,128)S(1)} %copy-done), custom_call_target="tpu_custom_call" | custom-call | tf_op jit(solution)/shard_map/forward/pallas_call | solution.py:451
  51.0 17.8 %all_to_all.22.back_ref = f32[64,8,128]{2,1,0:T(8,128)S(1)} all-to-all(f32[64,8,128]{2,1,0:T(8,128)S(1)} %get-tuple-element.21), channel_id=1, replica_groups=mesh['expert'=64,'dp'=4] {'expert'}, dimensions={0} | all-to-all | bytes 524288 | tf_op jit(solution)/shard_map/all_to_all | solution.py:464
  68.8 0.0 copy-done.5
  68.8 0.0 copy-done.7
  68.8 0.0 copy-done.8
  68.8 0.0 copy-done.9
  68.8 0.0 copy-done.10
  68.8 0.0 copy-done.11
  68.8 0.0 copy-done.12
  68.8 0.0 copy-done.13
  68.8 0.0 copy-done.14
  68.8 7.7 %rays.1 = (bf16[64,8,128]{2,1,0:T(8,128)(2,1)}, f32[1,128]{1,0:T(1,128)}, f32[16,64]{1,0:T(8,128)}, f32[16,64]{1,0:T(8,128)}, f32[16,64]{1,0:T(8,128)}) custom-call(f32[64,8,128]{2,1,0:T(8,128)S(1)} %all_to_all.22.back_ref, s32[32,128]{1,0:T(8,128)S(1)} %bitcast.23, s32[32,128]{1,0:T(8,128)S(1)} %bitcast.25, s32[1,128]{1,0:T(1,128)S(1)} %bitcast.27, ...), custom_call_target="tpu_custom_call" | custom-call | tf_op jit(solution)/shard_map/rays/pallas_call | solution.py:467
  76.6 5.7 %all-to-all-start.2 = ((bf16[64,8,128]{2,1,0:T(8,128)(2,1)}), bf16[64,8,128]{2,1,0:T(8,128)(2,1)S(1)}, u32[]{:S(2)}, u32[]{:S(2)}) async-start(bf16[64,8,128]{2,1,0:T(8,128)(2,1)} %get-tuple-element.24), calls=%async_computation.2 | async-start | bytes 262144 | tf_op jit(solution)/shard_map/all_to_all | solution.py:495
  82.2 9.9 %all-to-all-done.2.cot_in_ref = bf16[64,8,128]{2,1,0:T(8,128)(2,1)S(1)} async-done(((bf16[64,8,128]{2,1,0:T(8,128)(2,1)}), bf16[64,8,128]{2,1,0:T(8,128)(2,1)S(1)}, u32[]{:S(2)}, u32[]{:S(2)}) %all-to-all-start.2) | async-done | bytes 131104 | tf_op jit(solution)/shard_map/all_to_all | solution.py:495
  92.2 12.2 %backward.1 = (f32[424,256]{1,0:T(8,128)S(1)}, bf16[424,256]{1,0:T(8,128)(2,1)S(1)}, bf16[424,256]{1,0:T(8,128)(2,1)S(1)}, bf16[424,256]{1,0:T(8,128)(2,1)S(1)}) custom-call(s32[4]{0:T(128)S(1)} %and_select_fusion.order_ref, bf16[1024,384]{1,0:T(8,128)(2,1)S(1)} %bitcast.17, bf16[3,2,4,1024,256]{4,3,2,1,0:T(8,128)(2,1)} %get-tuple-element.23.acts_ref, ...), custom_call_target="tpu_custom_call" | custom-call | tf_op jit(solution)/shard_map/backward/pallas_call | solution.py:502
  104.4 3.3 %collective-permute-start = (bf16[424,256]{1,0:T(8,128)(2,1)S(1)}, bf16[424,256]{1,0:T(8,128)(2,1)S(1)}, u32[]{:S(2)}, u32[]{:S(2)}) collective-permute-start(bf16[424,256]{1,0:T(8,128)(2,1)S(1)} %get-tuple-element.26), channel_id=1, source_target_pairs={{0,2},{1,3},{2,0},{3,1},{4,6},{5,7},{6,4},{7,5},{8,10},{9,11},{10,... | collective-permute-start | bytes 651272 | tf_op jit(solution)/shard_map/ppermute | solution.py:529
  107.6 0.7 collective-permute-start.1
  108.3 2.6 %collective-permute-start.2 = (bf16[424,256]{1,0:T(8,128)(2,1)S(1)}, bf16[424,256]{1,0:T(8,128)(2,1)S(1)}, u32[]{:S(2)}, u32[]{:S(2)}) collective-permute-start(bf16[424,256]{1,0:T(8,128)(2,1)S(1)} %get-tuple-element.28), channel_id=1, source_target_pairs={{0,3},{1,0},{2,1},{3,2},{4,7},{5,4},{6,5},{7,6},{8,11},{9,8},{10,9... | collective-permute-start | bytes 651272 | tf_op jit(solution)/shard_map/ppermute | solution.py:529
  110.9 3.3 %collective-permute-done = bf16[424,256]{1,0:T(8,128)(2,1)S(1)} collective-permute-done((bf16[424,256]{1,0:T(8,128)(2,1)S(1)}, bf16[424,256]{1,0:T(8,128)(2,1)S(1)}, u32[]{:S(2)}, u32[]{:S(2)}) %collective-permute-start) | collective-permute-done | bytes 217120 | tf_op jit(solution)/shard_map/ppermute | solution.py:529
  114.1 3.8 %collective-permute-done.1 = bf16[424,256]{1,0:T(8,128)(2,1)S(1)} collective-permute-done((bf16[424,256]{1,0:T(8,128)(2,1)S(1)}, bf16[424,256]{1,0:T(8,128)(2,1)S(1)}, u32[]{:S(2)}, u32[]{:S(2)}) %collective-permute-start.1) | collective-permute-done | bytes 217120 | tf_op jit(solution)/shard_map/ppermute | solution.py:529
  118.0 0.3 collective-permute-done.2
  118.3 0.1 add_convert_fusion.own_ref
  118.4 2.8 %collective-permute-start.5 = (bf16[424,256]{1,0:T(8,128)(2,1)S(1)}, bf16[424,256]{1,0:T(8,128)(2,1)S(1)}, u32[]{:S(2)}, u32[]{:S(2)}) collective-permute-start(bf16[424,256]{1,0:T(8,128)(2,1)S(1)} %add_convert_fusion.own_ref), channel_id=1, source_target_pairs={{0,3},{1,0},{2,1},{3,2},{4,7},{5,4},{6,5},{7,6},{8,11},{9,8},{10,9... | collective-permute-start | bytes 651272 | tf_op jit(solution)/shard_map/ppermute | solution.py:529
  121.2 0.8 collective-permute-start.4
  122.0 0.2 collective-permute-start.3
  122.1 8.5 %collective-permute-done.5.third_ref = bf16[424,256]{1,0:T(8,128)(2,1)S(1)} collective-permute-done((bf16[424,256]{1,0:T(8,128)(2,1)S(1)}, bf16[424,256]{1,0:T(8,128)(2,1)S(1)}, u32[]{:S(2)}, u32[]{:S(2)}) %collective-permute-start.5) | collective-permute-done | bytes 217120 | tf_op jit(solution)/shard_map/ppermute | solution.py:529
  130.6 0.4 collective-permute-done.4.second_ref
  131.0 3.3 %collective-permute-done.3.first_ref = bf16[424,256]{1,0:T(8,128)(2,1)S(1)} collective-permute-done((bf16[424,256]{1,0:T(8,128)(2,1)S(1)}, bf16[424,256]{1,0:T(8,128)(2,1)S(1)}, u32[]{:S(2)}, u32[]{:S(2)}) %collective-permute-start.3) | collective-permute-done | bytes 217120 | tf_op jit(solution)/shard_map/ppermute | solution.py:529
  134.3 0.0 copy-done.1
  134.3 0.0 copy-done.2
  134.3 3.8 %adam.1 = (f32[1696,256]{1,0:T(8,128)}, f32[1696,256]{1,0:T(8,128)}, f32[1696,256]{1,0:T(8,128)}) custom-call(s32[4]{0:T(128)S(1)} %and_select_fusion.1.order_ref, bf16[424,256]{1,0:T(8,128)(2,1)S(1)} %add_convert_fusion.own_ref, bf16[424,256]{1,0:T(8,128)(2,1)S(1)} %collective-permute-done.3.first_ref, ...), custom_call_target="tpu_custom_call" | custom-call | tf_op jit(solution)/shard_map/adam/pallas_call | solution.py:540
  (6 shorter events, 0.0 us)
Async XLA Ops:
  0.6 42.8 %copy-start = (f32[2,848,256]{2,1,0:T(8,128)S(1)}, f32[2,848,256]{2,1,0:T(8,128)}, u32[]{:S(2)}) copy-start(f32[2,848,256]{2,1,0:T(8,128)} %params_ref.3) | copy-start | bytes 5210116
  0.6 1.2 copy-start.3
  1.8 0.7 copy-start.4
  2.5 0.7 copy-start.6
  43.4 25.4 %copy-start.5 = (s32[128,32]{0,1:T(8,128)S(1)}, s32[128,32]{0,1:T(8,128)}, u32[]{:S(2)}) copy-start(s32[128,32]{0,1:T(8,128)} %param.17) | copy-start | bytes 49156
  43.4 25.4 %copy-start.7 = (s32[128,32]{0,1:T(8,128)S(1)}, s32[128,32]{0,1:T(8,128)}, u32[]{:S(2)}) copy-start(s32[128,32]{0,1:T(8,128)} %param.18) | copy-start | bytes 49156
  43.4 25.4 %copy-start.8 = (f32[128,32]{0,1:T(8,128)S(1)}, f32[128,32]{0,1:T(8,128)}, u32[]{:S(2)}) copy-start(f32[128,32]{0,1:T(8,128)} %param.14) | copy-start | bytes 49156
  43.4 25.4 %copy-start.9 = (f32[16,64]{1,0:T(8,128)S(1)}, f32[16,64]{1,0:T(8,128)}, u32[]{:S(2)}) copy-start(f32[16,64]{1,0:T(8,128)} %code_ref.1) | copy-start | bytes 12292
  43.4 25.4 %copy-start.10 = (f32[16,64]{1,0:T(8,128)S(1)}, f32[16,64]{1,0:T(8,128)}, u32[]{:S(2)}) copy-start(f32[16,64]{1,0:T(8,128)} %first_ref.1) | copy-start | bytes 12292
  43.4 25.4 %copy-start.11 = (f32[16,64]{1,0:T(8,128)S(1)}, f32[16,64]{1,0:T(8,128)}, u32[]{:S(2)}) copy-start(f32[16,64]{1,0:T(8,128)} %second_ref.1) | copy-start | bytes 12292
  43.4 25.4 %copy-start.12 = (f32[3,128]{1,0:T(4,128)S(1)}, f32[3,128]{1,0:T(4,128)}, u32[]{:S(2)}) copy-start(f32[3,128]{1,0:T(4,128)} %targets_ref.1) | copy-start | bytes 4612
  43.4 25.4 %copy-start.13 = (s32[128]{0:T(128)S(1)}, s32[128]{0:T(128)}, u32[]{:S(2)}) copy-start(s32[128]{0:T(128)} %param.19) | copy-start | bytes 1540
  43.4 25.4 %copy-start.14 = (s32[128]{0:T(128)S(1)}, s32[128]{0:T(128)}, u32[]{:S(2)}) copy-start(s32[128]{0:T(128)} %param.16) | copy-start | bytes 1540
  76.6 15.6 %all-to-all-start.2 = ((bf16[64,8,128]{2,1,0:T(8,128)(2,1)}), bf16[64,8,128]{2,1,0:T(8,128)(2,1)S(1)}, u32[]{:S(2)}, u32[]{:S(2)}) async-start(bf16[64,8,128]{2,1,0:T(8,128)(2,1)} %get-tuple-element.24), calls=%async_computation.2 | async-start | bytes 262144 | tf_op jit(solution)/shard_map/all_to_all | solution.py:495
  92.2 42.1 %copy-start.1 = (f32[2,848,256]{2,1,0:T(8,128)S(1)}, f32[2,848,256]{2,1,0:T(8,128)}, u32[]{:S(2)}) copy-start(f32[2,848,256]{2,1,0:T(8,128)} %param.21) | copy-start | bytes 5210116
  92.2 42.1 %copy-start.2 = (f32[2,848,256]{2,1,0:T(8,128)S(1)}, f32[2,848,256]{2,1,0:T(8,128)}, u32[]{:S(2)}) copy-start(f32[2,848,256]{2,1,0:T(8,128)} %param.22) | copy-start | bytes 5210116
  104.4 9.8 %collective-permute-start = (bf16[424,256]{1,0:T(8,128)(2,1)S(1)}, bf16[424,256]{1,0:T(8,128)(2,1)S(1)}, u32[]{:S(2)}, u32[]{:S(2)}) collective-permute-start(bf16[424,256]{1,0:T(8,128)(2,1)S(1)} %get-tuple-element.26), channel_id=1, source_target_pairs={{0,2},{1,3},{2,0},{3,1},{4,6},{5,7},{6,4},{7,5},{8,10},{9,11},{10,... | collective-permute-start | bytes 651272 | tf_op jit(solution)/shard_map/ppermute | solution.py:529
  107.6 10.3 %collective-permute-start.1 = (bf16[424,256]{1,0:T(8,128)(2,1)S(1)}, bf16[424,256]{1,0:T(8,128)(2,1)S(1)}, u32[]{:S(2)}, u32[]{:S(2)}) collective-permute-start(bf16[424,256]{1,0:T(8,128)(2,1)S(1)} %get-tuple-element.27), channel_id=1, source_target_pairs={{0,1},{1,2},{2,3},{3,0},{4,5},{5,6},{6,7},{7,4},{8,9},{9,10},{10,1... | collective-permute-start | bytes 651272 | tf_op jit(solution)/shard_map/ppermute | solution.py:529
  108.3 10.0 %collective-permute-start.2 = (bf16[424,256]{1,0:T(8,128)(2,1)S(1)}, bf16[424,256]{1,0:T(8,128)(2,1)S(1)}, u32[]{:S(2)}, u32[]{:S(2)}) collective-permute-start(bf16[424,256]{1,0:T(8,128)(2,1)S(1)} %get-tuple-element.28), channel_id=1, source_target_pairs={{0,3},{1,0},{2,1},{3,2},{4,7},{5,4},{6,5},{7,6},{8,11},{9,8},{10,9... | collective-permute-start | bytes 651272 | tf_op jit(solution)/shard_map/ppermute | solution.py:529
  118.4 12.2 %collective-permute-start.5 = (bf16[424,256]{1,0:T(8,128)(2,1)S(1)}, bf16[424,256]{1,0:T(8,128)(2,1)S(1)}, u32[]{:S(2)}, u32[]{:S(2)}) collective-permute-start(bf16[424,256]{1,0:T(8,128)(2,1)S(1)} %add_convert_fusion.own_ref), channel_id=1, source_target_pairs={{0,3},{1,0},{2,1},{3,2},{4,7},{5,4},{6,5},{7,6},{8,11},{9,8},{10,9... | collective-permute-start | bytes 651272 | tf_op jit(solution)/shard_map/ppermute | solution.py:529
  121.2 9.8 %collective-permute-start.4 = (bf16[424,256]{1,0:T(8,128)(2,1)S(1)}, bf16[424,256]{1,0:T(8,128)(2,1)S(1)}, u32[]{:S(2)}, u32[]{:S(2)}) collective-permute-start(bf16[424,256]{1,0:T(8,128)(2,1)S(1)} %add_convert_fusion.own_ref), channel_id=1, source_target_pairs={{0,2},{1,3},{2,0},{3,1},{4,6},{5,7},{6,4},{7,5},{8,10},{9,11},{10,... | collective-permute-start | bytes 651272 | tf_op jit(solution)/shard_map/ppermute | solution.py:529
  122.0 12.3 %collective-permute-start.3 = (bf16[424,256]{1,0:T(8,128)(2,1)S(1)}, bf16[424,256]{1,0:T(8,128)(2,1)S(1)}, u32[]{:S(2)}, u32[]{:S(2)}) collective-permute-start(bf16[424,256]{1,0:T(8,128)(2,1)S(1)} %add_convert_fusion.own_ref), channel_id=1, source_target_pairs={{0,1},{1,2},{2,3},{3,0},{4,5},{5,6},{6,7},{7,4},{8,9},{9,10},{10,1... | collective-permute-start | bytes 651272 | tf_op jit(solution)/shard_map/ppermute | solution.py:529

commit v3 on v2

--- a/solution.py
+++ b/solution.py
@@ -1,3 +1,5 @@
+import functools
+
 import jax
 import jax.numpy as jnp
 from jax import lax
@@ -304,6 +306,7 @@
 
 
 def backward_kernel(
+    h,
     order_ref,
     x_ref,
     acts_ref,
@@ -323,21 +326,20 @@
 
     @pl.when(third == 0)
     def _():
-        weights_ref[...] = params_ref[...].astype(BF16)
+        weights_ref[...] = params_ref[0].astype(BF16)
         cot_ref[...] = cot_in_ref[...].astype(F32)
         total_ref[...] = jnp.zeros_like(total_ref)
-        for h in range(2):
-            lines = []
-            for c in range(4):
-                sums = jnp.sum(cot_ref[:, 3 + h * 2 + c // 2, :], axis=0, keepdims=True)
-                start = (c % 2) * CODE_WIDTH
-                line = sums[:, start : start + CODE_WIDTH]
-                lines.append(
-                    jnp.concatenate([line, jnp.zeros((1, NET_WIDTH - CODE_WIDTH), F32)], axis=1)
-                )
-            total_ref[h * PARAM_ROWS + HEAD_ROW : (h + 1) * PARAM_ROWS, :] = jnp.concatenate(
-                [jnp.zeros((4, NET_WIDTH), F32)] + lines + [jnp.zeros((8, NET_WIDTH), F32)], axis=0
+        lines = []
+        for c in range(4):
+            sums = jnp.sum(cot_ref[:, 3 + h * 2 + c // 2, :], axis=0, keepdims=True)
+            start = (c % 2) * CODE_WIDTH
+            line = sums[:, start : start + CODE_WIDTH]
+            lines.append(
+                jnp.concatenate([line, jnp.zeros((1, NET_WIDTH - CODE_WIDTH), F32)], axis=1)
             )
+        total_ref[HEAD_ROW:PARAM_ROWS, :] = jnp.concatenate(
+            [jnp.zeros((4, NET_WIDTH), F32)] + lines + [jnp.zeros((8, NET_WIDTH), F32)], axis=0
+        )
 
     cot = jnp.where(
         third == 0, cot_ref[:, 0, :], jnp.where(third == 1, cot_ref[:, 1, :], cot_ref[:, 2, :])
@@ -347,39 +349,32 @@
     spread = jnp.where(depth_match(rows), spread, 0.0).astype(BF16)
     lane = iota((1, 128), 1)
     wide_lane = iota((1, NET_WIDTH), 1)
-    for h in range(2):
-        head = weights_ref[h, HEAD_ROW:PARAM_ROWS, :].astype(F32)
-        last = acts_ref[0, h, LAYERS - 1]
-        outer = mul(spread, last, TN)[h * 64 : (h + 1) * 64]
-        head_grad = jnp.sum(outer.reshape(4, DEPTH, NET_WIDTH), axis=1)
-        bias_head = jnp.zeros((1, NET_WIDTH), F32)
-        for c in range(4):
-            value = jnp.sum(
-                jnp.where((lane >> 4) == h * 4 + c, sums, 0.0), axis=1, keepdims=True
-            )
-            bias_head = bias_head + jnp.where(wide_lane == c, value, 0.0)
-        up = mul(spread, head_tile(head, h))
-        bias_lines = [None] * LAYERS
-        for k in reversed(range(LAYERS)):
-            pre_grad = jnp.where(acts_ref[0, h, k].astype(F32) > 0, up, 0.0).astype(BF16)
-            bias_lines[k] = jnp.sum(pre_grad.astype(F32), axis=0, keepdims=True)
-            if k > 0:
-                start = h * PARAM_ROWS + ENC_WIDTH + (k - 1) * NET_WIDTH
-                total_ref[start : start + NET_WIDTH, :] += mul(
-                    acts_ref[0, h, k - 1], pre_grad, TN
-                )
-                up = mul(pre_grad, hidden_matrix(weights_ref, h, k), NT)
-            else:
-                start = h * PARAM_ROWS
-                total_ref[start : start + ENC_WIDTH, :] += mul(x_ref[...], pre_grad, TN)[
-                    h * ENC_WIDTH : (h + 1) * ENC_WIDTH
-                ]
-        total_ref[h * PARAM_ROWS + HEAD_ROW : (h + 1) * PARAM_ROWS, :] += jnp.concatenate(
-            [head_grad, jnp.zeros((4, NET_WIDTH), F32), bias_head]
-            + bias_lines
-            + [jnp.zeros((3, NET_WIDTH), F32)],
-            axis=0,
-        )
+    head = weights_ref[HEAD_ROW:PARAM_ROWS, :].astype(F32)
+    outer = mul(spread, acts_ref[0, 0, LAYERS - 1], TN)[h * 64 : (h + 1) * 64]
+    head_grad = jnp.sum(outer.reshape(4, DEPTH, NET_WIDTH), axis=1)
+    bias_head = jnp.zeros((1, NET_WIDTH), F32)
+    for c in range(4):
+        value = jnp.sum(jnp.where((lane >> 4) == h * 4 + c, sums, 0.0), axis=1, keepdims=True)
+        bias_head = bias_head + jnp.where(wide_lane == c, value, 0.0)
+    up = mul(spread, head_tile(head, h))
+    bias_lines = [None] * LAYERS
+    for k in reversed(range(LAYERS)):
+        pre_grad = jnp.where(acts_ref[0, 0, k].astype(F32) > 0, up, 0.0).astype(BF16)
+        bias_lines[k] = jnp.sum(pre_grad.astype(F32), axis=0, keepdims=True)
+        if k > 0:
+            start = ENC_WIDTH + (k - 1) * NET_WIDTH
+            total_ref[start : start + NET_WIDTH, :] += mul(acts_ref[0, 0, k - 1], pre_grad, TN)
+            up = mul(pre_grad, weights_ref[start : start + NET_WIDTH, :], NT)
+        else:
+            total_ref[0:ENC_WIDTH, :] += mul(x_ref[...], pre_grad, TN)[
+                h * ENC_WIDTH : (h + 1) * ENC_WIDTH
+            ]
+    total_ref[HEAD_ROW:PARAM_ROWS, :] += jnp.concatenate(
+        [head_grad, jnp.zeros((4, NET_WIDTH), F32), bias_head]
+        + bias_lines
+        + [jnp.zeros((3, NET_WIDTH), F32)],
+        axis=0,
+    )
 
     @pl.when(third == THIRDS - 1)
     def _():
@@ -390,20 +385,34 @@
 
 
 def adam_kernel(
-    order_ref, own_ref, first_ref, second_ref, third_ref, *refs
+    order_ref,
+    own_ref,
+    first_ref,
+    second_ref,
+    third_ref,
+    param_ref,
+    one_ref,
+    two_ref,
+    *refs,
 ):
     step = pl.program_id(0)
-    param_ref, one_ref, two_ref, new_param_ref, new_one_ref, new_two_ref = refs
+    new_param_ref, new_one_ref, new_two_ref = refs[-3:]
     for k, share_ref in enumerate((own_ref, first_ref, second_ref, third_ref)):
 
         @pl.when(step == k)
         def _():
             new_param, new_one, new_two = adam_update(
-                param_ref[...], share_ref[...].astype(F32), one_ref[...], two_ref[...]
+                param_ref[0], share_ref[...].astype(F32), one_ref[0], two_ref[0]
             )
-            new_param_ref[...] = new_param
-            new_one_ref[...] = new_one
-            new_two_ref[...] = new_two
+            new_param_ref[0] = new_param
+            new_one_ref[0] = new_one
+            new_two_ref[0] = new_two
+
+
+def cost(micros):
+    return pl.CostEstimate(
+        flops=int(micros * 1e9), bytes_accessed=int(micros * 3e6), transcendentals=0
+    )
 
 
 def limits(mib=48):
@@ -495,70 +504,79 @@
     cot_in = lax.all_to_all(cot_out, "expert", split_axis=0, concat_axis=0, tiled=True)
 
     copies = lax.axis_size("dp")
-    quarter = 2 * PARAM_ROWS // copies
+    quarter = -(-PARAM_ROWS // (8 * copies)) * 8
     turns = jnp.arange(copies, dtype=jnp.int32)
     position = lax.axis_index("dp")
     lent = lambda *dims: pl.BlockSpec(dims, lambda i, order: (0,) * len(dims))
-    shares = pl.pallas_call(
-        backward_kernel,
-        grid_spec=pltpu.PrefetchScalarGridSpec(
-            num_scalar_prefetch=1,
-            grid=(THIRDS,),
-            in_specs=[
-                pl.BlockSpec((places, 128), lambda i, order: (0, i)),
-                pl.BlockSpec(
-                    (1, 2, LAYERS, places, NET_WIDTH), lambda i, order: (i, 0, 0, 0, 0)
-                ),
-                lent(groups, 8, 128),
-                lent(2, PARAM_ROWS, NET_WIDTH),
-            ],
-            out_specs=[lent(quarter, NET_WIDTH)] * 4,
-            scratch_shapes=[
-                pltpu.VMEM((2, PARAM_ROWS, NET_WIDTH), BF16),
-                pltpu.VMEM((2 * PARAM_ROWS, NET_WIDTH), F32),
-                pltpu.VMEM((groups, 8, 128), F32),
-            ],
-        ),
-        out_shape=[shape_of((quarter, NET_WIDTH), F32)]
-        + [shape_of((quarter, NET_WIDTH), BF16)] * 3,
-        compiler_params=limits(),
-        name="backward",
-    )((position + turns) % copies, arrived, acts, cot_in, params)
 
     def send(value, distance):
         return lax.ppermute(value, "dp", [(i, (i + distance) % copies) for i in range(copies)])
 
-    share = shares[0]
-    for k in (2, 1, 3):
-        share = share + send(shares[k], k).astype(F32)
-    share = share.astype(BF16)
-    others = [None, None, None]
-    for k in (2, 1, 3):
-        others[k - 1] = send(share, k)
-    flat = (2 * PARAM_ROWS, NET_WIDTH)
-    by_order = pl.BlockSpec((quarter, NET_WIDTH), lambda i, order: (order[i], 0))
-    new_params, new_first, new_second = pl.pallas_call(
-        adam_kernel,
-        grid_spec=pltpu.PrefetchScalarGridSpec(
-            num_scalar_prefetch=1,
-            grid=(copies,),
-            in_specs=[lent(quarter, NET_WIDTH)] * 4 + [by_order] * 3,
-            out_specs=[by_order] * 3,
-        ),
-        out_shape=[shape_of(flat, F32)] * 3,
-        compiler_params=limits(),
-        name="adam",
-    )(
-        (position - turns) % copies,
-        share,
-        *others,
-        params.reshape(flat),
-        first_moment.reshape(flat),
-        second_moment.reshape(flat),
-    )
-    new_params, new_first, new_second = (
-        value.reshape(params.shape) for value in (new_params, new_first, new_second)
-    )
+    def gradient(h):
+        return pl.pallas_call(
+            functools.partial(backward_kernel, h),
+            grid_spec=pltpu.PrefetchScalarGridSpec(
+                num_scalar_prefetch=1,
+                grid=(THIRDS,),
+                in_specs=[
+                    pl.BlockSpec((places, 128), lambda i, order: (0, i)),
+                    pl.BlockSpec(
+                        (1, 1, LAYERS, places, NET_WIDTH), lambda i, order: (i, h, 0, 0, 0)
+                    ),
+                    lent(groups, 8, 128),
+                    pl.BlockSpec((1, PARAM_ROWS, NET_WIDTH), lambda i, order: (h, 0, 0)),
+                ],
+                out_specs=[lent(quarter, NET_WIDTH)] * 4,
+                scratch_shapes=[
+                    pltpu.VMEM((PARAM_ROWS, NET_WIDTH), BF16),
+                    pltpu.VMEM((copies * quarter, NET_WIDTH), F32),
+                    pltpu.VMEM((groups, 8, 128), F32),
+                ],
+            ),
+            out_shape=[shape_of((quarter, NET_WIDTH), F32)]
+            + [shape_of((quarter, NET_WIDTH), BF16)] * 3,
+            compiler_params=limits(),
+            cost_estimate=cost(6.0),
+            name="backward",
+        )((position + turns) % copies, arrived, acts, cot_in, params)
+
+    def collect(shares):
+        share = shares[0]
+        for k in (2, 1, 3):
+            share = share + send(shares[k], k).astype(F32)
+        share = share.astype(BF16)
+        behind, ahead = send(share, 1), send(share, 3)
+        return share, behind, send(ahead, 3), ahead
+
+    def update(h, pieces, earlier):
+        block = pl.BlockSpec((1, quarter, NET_WIDTH), lambda i, order: (h, order[i], 0))
+        return pl.pallas_call(
+            adam_kernel,
+            grid_spec=pltpu.PrefetchScalarGridSpec(
+                num_scalar_prefetch=1,
+                grid=(copies,),
+                in_specs=[lent(quarter, NET_WIDTH)] * 4
+                + [block] * 3
+                + [pl.BlockSpec(memory_space=pl.ANY)] * len(earlier),
+                out_specs=[block] * 3,
+            ),
+            out_shape=[shape_of(params.shape, F32)] * 3,
+            input_output_aliases={8 + i: i for i in range(len(earlier))},
+            compiler_params=limits(),
+            cost_estimate=cost(2.0),
+            name="adam",
+        )(
+            (position - turns) % copies,
+            *pieces,
+            params,
+            first_moment,
+            second_moment,
+            *earlier,
+        )
+
+    pieces = [collect(gradient(h)) for h in range(2)]
+    updated = update(0, pieces[0], ())
+    new_params, new_first, new_second = update(1, pieces[1], updated)
     return (
         loss.reshape(RAYS),
         new_params,

time: 141 us -> 137 us (0.972); the launches traced: 138 us -> 136 us
  waiting for transfers between devices: 29.5 us -> 14.7 us
  starting transfers between devices: 15.9 us -> 24 us
  Pallas kernels: 36.3 us -> 40.3 us
    ppermute x6 -> x12, waiting for transfers between devices: 19.6 us -> 4.82 us  [send(): lax.ppermute(value, 'dp', [(i, (i + distance) % copies) for i in range(co...]
    ppermute x6 -> x12, starting transfers between devices: 10.2 us -> 18.4 us  [send(): lax.ppermute(value, 'dp', [(i, (i + distance) % copies) for i in range(co...]
    pallas_call x2 -> x4, Pallas kernels: 15.9 us -> 20 us  [the longest x2 14.1 us: gradient(): pl.pallas_call(functools.partial(backward_kernel, h), grid_spec=pltpu.Pre...]
  transfers between devices with their start and end apart: 7 -> 13, of which waited for: 7 -> 3; matrix products, arithmetic and copies ran while one was open for 0% -> 0% of each run, Pallas kernels for 0% -> 7%
where the time goes in v3:
time: 137 us; the launch traced here: 136 us
  blocking collectives  52.8 us (39%)
  Pallas kernels  40.3 us (29%)
  starting transfers between devices  24 us (18%)
  waiting for transfers between devices  14.7 us (11%)
  local copies, waits for them, and re-layouts  2.65 us (2%)
    all_to_all x1, blocking collectives, shards(): lax.all_to_all(outgoing, 'expert', split_axis=0, concat_axis=0, tiled=True)  35 us
    ppermute x12, starting transfers between devices, send(): lax.ppermute(value, 'dp', [(i, (i + distance) % copies) for i in range(co...  18.4 us
    all_to_all x1, blocking collectives, shards(): lax.all_to_all(raw_out, 'expert', split_axis=0, concat_axis=0, tiled=True)  17.8 us
    pallas_call x2, Pallas kernels, gradient(): pl.pallas_call(functools.partial(backward_kernel, h), grid_spec=pltpu.Pre...  14.1 us
    all_to_all x1, waiting for transfers between devices, shards(): lax.all_to_all(cot_out, 'expert', split_axis=0, concat_axis=0, tiled=True)  9.93 us
    pallas_call x1, Pallas kernels, shards(): pl.pallas_call(ray_kernel, out_shape=[shape_of((groups, 8, 128), BF16), s...  7.71 us
    pallas_call x1, Pallas kernels, shards(): pl.pallas_call(forward_kernel, grid=(THIRDS,), in_specs=[third_rows, whol...  7.55 us
    pallas_call x2, Pallas kernels, update(): pl.pallas_call(adam_kernel, grid_spec=pltpu.PrefetchScalarGridSpec(num_sc...  5.81 us
  transfers between devices with their start and end apart: 13, of which 3 were waited for; matrix products, arithmetic and copies ran while one was open for 0% of the time, Pallas kernels for 7%

profile of v3, /device:TPU:2, one launch (start us, length us, event | category | flops | bytes accessed | tf_op | source)
XLA Modules:
  0.0 135.5 jit_solution(9708348053035022572)
XLA Ops:
  0.7 1.2 copy-done.3
  1.8 0.7 copy-done.4
  2.5 0.7 copy-done.6
  3.2 5.1 %dispatch.1 = bf16[1024,384]{1,0:T(8,128)(2,1)S(1)} custom-call(bf16[32,64,128]{2,1,0:T(8,128)(2,1)S(1)} %bitcast.13, s32[32,128]{1,0:T(8,128)S(1)} %bitcast.14, s32[32,128]{1,0:T(8,128)S(1)} %bitcast.16), custom_call_target="tpu_custom_call" | custom-call | tf_op jit(solution)/shard_map/dispatch/pallas_call | solution.py:445
  8.4 35.0 %all_to_all.21 = bf16[64,16,384]{2,1,0:T(8,128)(2,1)S(1)} all-to-all(bf16[64,16,384]{2,1,0:T(8,128)(2,1)S(1)} %bitcast.12), channel_id=1, replica_groups=mesh['expert'=64,'dp'=4] {'expert'}, dimensions={0} | all-to-all | bytes 1572864 | tf_op jit(solution)/shard_map/all_to_all | solution.py:455
  43.4 0.0 copy-start.10
  43.4 0.0 copy-start.11
  43.4 0.0 copy-start.12
  43.4 0.0 copy-start.13
  43.4 0.0 copy-start.14
  43.4 7.6 %forward.1 = (bf16[3,2,4,1024,256]{4,3,2,1,0:T(8,128)(2,1)}, f32[64,8,128]{2,1,0:T(8,128)S(1)}) custom-call(bf16[1024,384]{1,0:T(8,128)(2,1)S(1)} %bitcast.9, f32[2,848,256]{2,1,0:T(8,128)S(1)} %copy-done), custom_call_target="tpu_custom_call" | custom-call | tf_op jit(solution)/shard_map/forward/pallas_call | solution.py:460
  51.0 17.8 %all_to_all.22.back_ref = f32[64,8,128]{2,1,0:T(8,128)S(1)} all-to-all(f32[64,8,128]{2,1,0:T(8,128)S(1)} %get-tuple-element.28), channel_id=1, replica_groups=mesh['expert'=64,'dp'=4] {'expert'}, dimensions={0} | all-to-all | bytes 524288 | tf_op jit(solution)/shard_map/all_to_all | solution.py:473
  68.8 0.0 copy-done.5
  68.9 7.7 %rays.1 = (bf16[64,8,128]{2,1,0:T(8,128)(2,1)}, f32[1,128]{1,0:T(1,128)}, f32[16,64]{1,0:T(8,128)}, f32[16,64]{1,0:T(8,128)}, f32[16,64]{1,0:T(8,128)}) custom-call(f32[64,8,128]{2,1,0:T(8,128)S(1)} %all_to_all.22.back_ref, s32[32,128]{1,0:T(8,128)S(1)} %bitcast.15, s32[32,128]{1,0:T(8,128)S(1)} %bitcast.17, s32[1,128]{1,0:T(1,128)S(1)} %bitcast.19, ...), custom_call_target="tpu_custom_call" | custom-call | tf_op jit(solution)/shard_map/rays/pallas_call | solution.py:476
  76.6 5.7 %all-to-all-start.2 = ((bf16[64,8,128]{2,1,0:T(8,128)(2,1)}), bf16[64,8,128]{2,1,0:T(8,128)(2,1)S(1)}, u32[]{:S(2)}, u32[]{:S(2)}) async-start(bf16[64,8,128]{2,1,0:T(8,128)(2,1)} %get-tuple-element.31), calls=%async_computation.2 | async-start | bytes 262144 | tf_op jit(solution)/shard_map/all_to_all | solution.py:504
  82.3 9.9 %all-to-all-done.2.cot_in_ref = bf16[64,8,128]{2,1,0:T(8,128)(2,1)S(1)} async-done(((bf16[64,8,128]{2,1,0:T(8,128)(2,1)}), bf16[64,8,128]{2,1,0:T(8,128)(2,1)S(1)}, u32[]{:S(2)}, u32[]{:S(2)}) %all-to-all-start.2) | async-done | bytes 131104 | tf_op jit(solution)/shard_map/all_to_all | solution.py:504
  92.2 7.1 %backward.3 = (f32[216,256]{1,0:T(8,128)S(1)}, bf16[216,256]{1,0:T(8,128)(2,1)S(1)}, bf16[216,256]{1,0:T(8,128)(2,1)S(1)}, bf16[216,256]{1,0:T(8,128)(2,1)S(1)}) custom-call(s32[4]{0:T(128)S(1)} %and_select_fusion.order_ref, bf16[1024,384]{1,0:T(8,128)(2,1)S(1)} %bitcast.10, bf16[3,2,4,1024,256]{4,3,2,1,0:T(8,128)(2,1)} %get-tuple-element.30.acts_ref, ...), custom_call_target="tpu_custom_call" | custom-call | flops 6000000000 | bytes 18000000 | tf_op jit(solution)/shard_map/backward/pallas_call | solution.py:516
  99.3 3.1 %collective-permute-start.8 = (bf16[216,256]{1,0:T(8,128)(2,1)S(1)}, bf16[216,256]{1,0:T(8,128)(2,1)S(1)}, u32[]{:S(2)}, u32[]{:S(2)}) collective-permute-start(bf16[216,256]{1,0:T(8,128)(2,1)S(1)} %get-tuple-element.39), channel_id=1, source_target_pairs={{0,3},{1,0},{2,1},{3,2},{4,7},{5,4},{6,5},{7,6},{8,11},{9,8},{10,9... | collective-permute-start | bytes 331784 | tf_op jit(solution)/shard_map/ppermute | solution.py:513
  102.4 0.0 collective-permute-start.7
  102.4 2.2 %collective-permute-start.6 = (bf16[216,256]{1,0:T(8,128)(2,1)S(1)}, bf16[216,256]{1,0:T(8,128)(2,1)S(1)}, u32[]{:S(2)}, u32[]{:S(2)}) collective-permute-start(bf16[216,256]{1,0:T(8,128)(2,1)S(1)} %get-tuple-element.37), channel_id=1, source_target_pairs={{0,2},{1,3},{2,0},{3,1},{4,6},{5,7},{6,4},{7,5},{8,10},{9,11},{10,... | collective-permute-start | bytes 331784 | tf_op jit(solution)/shard_map/ppermute | solution.py:513
  104.6 7.1 %backward.2 = (f32[216,256]{1,0:T(8,128)S(1)}, bf16[216,256]{1,0:T(8,128)(2,1)S(1)}, bf16[216,256]{1,0:T(8,128)(2,1)S(1)}, bf16[216,256]{1,0:T(8,128)(2,1)S(1)}) custom-call(s32[4]{0:T(128)S(1)} %and_select_fusion.order_ref, bf16[1024,384]{1,0:T(8,128)(2,1)S(1)} %bitcast.11, bf16[3,2,4,1024,256]{4,3,2,1,0:T(8,128)(2,1)} %get-tuple-element.30.acts_ref, ...), custom_call_target="tpu_custom_call" | custom-call | flops 6000000000 | bytes 18000000 | tf_op jit(solution)/shard_map/backward/pallas_call | solution.py:516
  111.7 1.4 %collective-permute-start.2 = (bf16[216,256]{1,0:T(8,128)(2,1)S(1)}, bf16[216,256]{1,0:T(8,128)(2,1)S(1)}, u32[]{:S(2)}, u32[]{:S(2)}) collective-permute-start(bf16[216,256]{1,0:T(8,128)(2,1)S(1)} %get-tuple-element.35), channel_id=1, source_target_pairs={{0,3},{1,0},{2,1},{3,2},{4,7},{5,4},{6,5},{7,6},{8,11},{9,8},{10,9... | collective-permute-start | bytes 331784 | tf_op jit(solution)/shard_map/ppermute | solution.py:513
  113.1 0.7 collective-permute-start.1
  113.8 0.0 collective-permute-done.8
  113.8 1.9 %collective-permute-start = (bf16[216,256]{1,0:T(8,128)(2,1)S(1)}, bf16[216,256]{1,0:T(8,128)(2,1)S(1)}, u32[]{:S(2)}, u32[]{:S(2)}) collective-permute-start(bf16[216,256]{1,0:T(8,128)(2,1)S(1)} %get-tuple-element.33), channel_id=1, source_target_pairs={{0,2},{1,3},{2,0},{3,1},{4,6},{5,7},{6,4},{7,5},{8,10},{9,11},{10,... | collective-permute-start | bytes 331784 | tf_op jit(solution)/shard_map/ppermute | solution.py:513
  115.7 0.0 collective-permute-done.7
  115.7 0.0 collective-permute-done.6
  115.7 0.1 add_convert_fusion.own_ref
  115.8 1.6 %collective-permute-start.9 = (bf16[216,256]{1,0:T(8,128)(2,1)S(1)}, bf16[216,256]{1,0:T(8,128)(2,1)S(1)}, u32[]{:S(2)}, u32[]{:S(2)}) collective-permute-start(bf16[216,256]{1,0:T(8,128)(2,1)S(1)} %add_convert_fusion.own_ref), channel_id=1, source_target_pairs={{0,1},{1,2},{2,3},{3,0},{4,5},{5,6},{6,7},{7,4},{8,9},{9,10},{10,1... | collective-permute-start | bytes 331784 | tf_op jit(solution)/shard_map/ppermute | solution.py:513
  117.4 1.7 %collective-permute-start.10 = (bf16[216,256]{1,0:T(8,128)(2,1)S(1)}, bf16[216,256]{1,0:T(8,128)(2,1)S(1)}, u32[]{:S(2)}, u32[]{:S(2)}) collective-permute-start(bf16[216,256]{1,0:T(8,128)(2,1)S(1)} %add_convert_fusion.own_ref), channel_id=1, source_target_pairs={{0,3},{1,0},{2,1},{3,2},{4,7},{5,4},{6,5},{7,6},{8,11},{9,8},{10,9... | collective-permute-start | bytes 331784 | tf_op jit(solution)/shard_map/ppermute | solution.py:513
  119.1 0.0 collective-permute-done.2
  119.1 2.9 %collective-permute-done.1 = bf16[216,256]{1,0:T(8,128)(2,1)S(1)} collective-permute-done((bf16[216,256]{1,0:T(8,128)(2,1)S(1)}, bf16[216,256]{1,0:T(8,128)(2,1)S(1)}, u32[]{:S(2)}, u32[]{:S(2)}) %collective-permute-start.1) | collective-permute-done | bytes 110624 | tf_op jit(solution)/shard_map/ppermute | solution.py:513
  122.0 0.0 collective-permute-done
  122.0 0.1 add_convert_fusion.1.own_ref
  122.1 1.5 %collective-permute-start.4 = (bf16[216,256]{1,0:T(8,128)(2,1)S(1)}, bf16[216,256]{1,0:T(8,128)(2,1)S(1)}, u32[]{:S(2)}, u32[]{:S(2)}) collective-permute-start(bf16[216,256]{1,0:T(8,128)(2,1)S(1)} %add_convert_fusion.1.own_ref), channel_id=1, source_target_pairs={{0,3},{1,0},{2,1},{3,2},{4,7},{5,4},{6,5},{7,6},{8,11},{9,8},{10,9... | collective-permute-start | bytes 331784 | tf_op jit(solution)/shard_map/ppermute | solution.py:513
  123.6 0.0 collective-permute-done.10.third_ref
  123.6 2.3 %collective-permute-start.11 = (bf16[216,256]{1,0:T(8,128)(2,1)S(1)}, bf16[216,256]{1,0:T(8,128)(2,1)S(1)}, u32[]{:S(2)}, u32[]{:S(2)}) collective-permute-start(bf16[216,256]{1,0:T(8,128)(2,1)S(1)} %collective-permute-done.10.third_ref), channel_id=1, source_target_pairs={{0,3},{1,0},{2,1},{3,2},{4,7},{5,4},{6,5},{7,6},{8,11},{9,8},{10,9... | collective-permute-start | bytes 331784 | tf_op jit(solution)/shard_map/ppermute | solution.py:513
  125.9 0.0 collective-permute-start.3
  125.9 1.9 %collective-permute-done.4.third_ref = bf16[216,256]{1,0:T(8,128)(2,1)S(1)} collective-permute-done((bf16[216,256]{1,0:T(8,128)(2,1)S(1)}, bf16[216,256]{1,0:T(8,128)(2,1)S(1)}, u32[]{:S(2)}, u32[]{:S(2)}) %collective-permute-start.4) | collective-permute-done | bytes 110624 | tf_op jit(solution)/shard_map/ppermute | solution.py:513
  127.8 1.9 %collective-permute-start.5 = (bf16[216,256]{1,0:T(8,128)(2,1)S(1)}, bf16[216,256]{1,0:T(8,128)(2,1)S(1)}, u32[]{:S(2)}, u32[]{:S(2)}) collective-permute-start(bf16[216,256]{1,0:T(8,128)(2,1)S(1)} %collective-permute-done.4.third_ref), channel_id=1, source_target_pairs={{0,3},{1,0},{2,1},{3,2},{4,7},{5,4},{6,5},{7,6},{8,11},{9,8},{10,9... | collective-permute-start | bytes 331784 | tf_op jit(solution)/shard_map/ppermute | solution.py:513
  129.7 0.0 collective-permute-done.9.first_ref
  129.7 0.0 collective-permute-done.11.second_ref
  129.7 0.0 copy-done.1
  129.7 0.0 copy-done.2
  129.7 2.9 %adam.2 = (f32[2,848,256]{2,1,0:T(8,128)}, f32[2,848,256]{2,1,0:T(8,128)}, f32[2,848,256]{2,1,0:T(8,128)}) custom-call(s32[4]{0:T(128)S(1)} %and_select_fusion.1.order_ref, bf16[216,256]{1,0:T(8,128)(2,1)S(1)} %add_convert_fusion.own_ref, bf16[216,256]{1,0:T(8,128)(2,1)S(1)} %collective-permute-done.9.first_ref, ...), custom_call_target="tpu_custom_call" | custom-call | flops 2000000000 | bytes 6000000 | tf_op jit(solution)/shard_map/adam/pallas_call | solution.py:553
  132.6 0.0 collective-permute-done.3.first_ref
  132.6 0.0 collective-permute-done.5.second_ref
  132.6 2.9 %adam.3 = (f32[2,848,256]{2,1,0:T(8,128)}, f32[2,848,256]{2,1,0:T(8,128)}, f32[2,848,256]{2,1,0:T(8,128)}) custom-call(s32[4]{0:T(128)S(1)} %and_select_fusion.1.order_ref, bf16[216,256]{1,0:T(8,128)(2,1)S(1)} %add_convert_fusion.1.own_ref, ...), custom_call_target="tpu_custom_call", output_to_operand_aliasing={{0}: (8, {}), {1}: (9, {}), {2}: (10, {})} | custom-call | flops 2000000000 | bytes 6000000 | tf_op jit(solution)/shard_map/adam/pallas_call | solution.py:553
  (21 shorter events, 0.1 us)
Async XLA Ops:
  0.6 42.8 %copy-start = (f32[2,848,256]{2,1,0:T(8,128)S(1)}, f32[2,848,256]{2,1,0:T(8,128)}, u32[]{:S(2)}) copy-start(f32[2,848,256]{2,1,0:T(8,128)} %param_ref.3) | copy-start | bytes 5210116
  0.6 1.2 copy-start.3
  1.8 0.7 copy-start.4
  2.5 0.7 copy-start.6
  43.4 25.5 %copy-start.5 = (s32[128,32]{0,1:T(8,128)S(1)}, s32[128,32]{0,1:T(8,128)}, u32[]{:S(2)}) copy-start(s32[128,32]{0,1:T(8,128)} %param.17) | copy-start | bytes 49156
  43.4 25.5 %copy-start.7 = (s32[128,32]{0,1:T(8,128)S(1)}, s32[128,32]{0,1:T(8,128)}, u32[]{:S(2)}) copy-start(s32[128,32]{0,1:T(8,128)} %param.18) | copy-start | bytes 49156
  43.4 25.5 %copy-start.8 = (f32[128,32]{0,1:T(8,128)S(1)}, f32[128,32]{0,1:T(8,128)}, u32[]{:S(2)}) copy-start(f32[128,32]{0,1:T(8,128)} %param.14) | copy-start | bytes 49156
  43.4 25.5 %copy-start.9 = (f32[16,64]{1,0:T(8,128)S(1)}, f32[16,64]{1,0:T(8,128)}, u32[]{:S(2)}) copy-start(f32[16,64]{1,0:T(8,128)} %code_ref.1) | copy-start | bytes 12292
  43.4 25.5 %copy-start.10 = (f32[16,64]{1,0:T(8,128)S(1)}, f32[16,64]{1,0:T(8,128)}, u32[]{:S(2)}) copy-start(f32[16,64]{1,0:T(8,128)} %first_ref.1) | copy-start | bytes 12292
  43.4 25.5 %copy-start.11 = (f32[16,64]{1,0:T(8,128)S(1)}, f32[16,64]{1,0:T(8,128)}, u32[]{:S(2)}) copy-start(f32[16,64]{1,0:T(8,128)} %second_ref.1) | copy-start | bytes 12292
  43.4 25.5 %copy-start.12 = (f32[3,128]{1,0:T(4,128)S(1)}, f32[3,128]{1,0:T(4,128)}, u32[]{:S(2)}) copy-start(f32[3,128]{1,0:T(4,128)} %targets_ref.1) | copy-start | bytes 4612
  43.4 25.5 %copy-start.13 = (s32[128]{0:T(128)S(1)}, s32[128]{0:T(128)}, u32[]{:S(2)}) copy-start(s32[128]{0:T(128)} %param.19) | copy-start | bytes 1540
  43.4 25.5 %copy-start.14 = (s32[128]{0:T(128)S(1)}, s32[128]{0:T(128)}, u32[]{:S(2)}) copy-start(s32[128]{0:T(128)} %param.16) | copy-start | bytes 1540
  76.6 15.6 %all-to-all-start.2 = ((bf16[64,8,128]{2,1,0:T(8,128)(2,1)}), bf16[64,8,128]{2,1,0:T(8,128)(2,1)S(1)}, u32[]{:S(2)}, u32[]{:S(2)}) async-start(bf16[64,8,128]{2,1,0:T(8,128)(2,1)} %get-tuple-element.31), calls=%async_computation.2 | async-start | bytes 262144 | tf_op jit(solution)/shard_map/all_to_all | solution.py:504
  99.3 14.5 %collective-permute-start.8 = (bf16[216,256]{1,0:T(8,128)(2,1)S(1)}, bf16[216,256]{1,0:T(8,128)(2,1)S(1)}, u32[]{:S(2)}, u32[]{:S(2)}) collective-permute-start(bf16[216,256]{1,0:T(8,128)(2,1)S(1)} %get-tuple-element.39), channel_id=1, source_target_pairs={{0,3},{1,0},{2,1},{3,2},{4,7},{5,4},{6,5},{7,6},{8,11},{9,8},{10,9... | collective-permute-start | bytes 331784 | tf_op jit(solution)/shard_map/ppermute | solution.py:513
  102.4 13.3 %collective-permute-start.7 = (bf16[216,256]{1,0:T(8,128)(2,1)S(1)}, bf16[216,256]{1,0:T(8,128)(2,1)S(1)}, u32[]{:S(2)}, u32[]{:S(2)}) collective-permute-start(bf16[216,256]{1,0:T(8,128)(2,1)S(1)} %get-tuple-element.38), channel_id=1, source_target_pairs={{0,1},{1,2},{2,3},{3,0},{4,5},{5,6},{6,7},{7,4},{8,9},{9,10},{10,1... | collective-permute-start | bytes 331784 | tf_op jit(solution)/shard_map/ppermute | solution.py:513
  102.4 27.3 %copy-start.1 = (f32[2,848,256]{2,1,0:T(8,128)S(1)}, f32[2,848,256]{2,1,0:T(8,128)}, u32[]{:S(2)}) copy-start(f32[2,848,256]{2,1,0:T(8,128)} %one_ref.3) | copy-start | bytes 5210116
  102.4 27.3 %copy-start.2 = (f32[2,848,256]{2,1,0:T(8,128)S(1)}, f32[2,848,256]{2,1,0:T(8,128)}, u32[]{:S(2)}) copy-start(f32[2,848,256]{2,1,0:T(8,128)} %two_ref.3) | copy-start | bytes 5210116
  102.4 13.3 %collective-permute-start.6 = (bf16[216,256]{1,0:T(8,128)(2,1)S(1)}, bf16[216,256]{1,0:T(8,128)(2,1)S(1)}, u32[]{:S(2)}, u32[]{:S(2)}) collective-permute-start(bf16[216,256]{1,0:T(8,128)(2,1)S(1)} %get-tuple-element.37), channel_id=1, source_target_pairs={{0,2},{1,3},{2,0},{3,1},{4,6},{5,7},{6,4},{7,5},{8,10},{9,11},{10,... | collective-permute-start | bytes 331784 | tf_op jit(solution)/shard_map/ppermute | solution.py:513
  111.7 7.4 %collective-permute-start.2 = (bf16[216,256]{1,0:T(8,128)(2,1)S(1)}, bf16[216,256]{1,0:T(8,128)(2,1)S(1)}, u32[]{:S(2)}, u32[]{:S(2)}) collective-permute-start(bf16[216,256]{1,0:T(8,128)(2,1)S(1)} %get-tuple-element.35), channel_id=1, source_target_pairs={{0,3},{1,0},{2,1},{3,2},{4,7},{5,4},{6,5},{7,6},{8,11},{9,8},{10,9... | collective-permute-start | bytes 331784 | tf_op jit(solution)/shard_map/ppermute | solution.py:513
  113.1 8.9 %collective-permute-start.1 = (bf16[216,256]{1,0:T(8,128)(2,1)S(1)}, bf16[216,256]{1,0:T(8,128)(2,1)S(1)}, u32[]{:S(2)}, u32[]{:S(2)}) collective-permute-start(bf16[216,256]{1,0:T(8,128)(2,1)S(1)} %get-tuple-element.34), channel_id=1, source_target_pairs={{0,1},{1,2},{2,3},{3,0},{4,5},{5,6},{6,7},{7,4},{8,9},{9,10},{10,1... | collective-permute-start | bytes 331784 | tf_op jit(solution)/shard_map/ppermute | solution.py:513
  113.8 8.2 %collective-permute-start = (bf16[216,256]{1,0:T(8,128)(2,1)S(1)}, bf16[216,256]{1,0:T(8,128)(2,1)S(1)}, u32[]{:S(2)}, u32[]{:S(2)}) collective-permute-start(bf16[216,256]{1,0:T(8,128)(2,1)S(1)} %get-tuple-element.33), channel_id=1, source_target_pairs={{0,2},{1,3},{2,0},{3,1},{4,6},{5,7},{6,4},{7,5},{8,10},{9,11},{10,... | collective-permute-start | bytes 331784 | tf_op jit(solution)/shard_map/ppermute | solution.py:513
  115.8 13.9 %collective-permute-start.9 = (bf16[216,256]{1,0:T(8,128)(2,1)S(1)}, bf16[216,256]{1,0:T(8,128)(2,1)S(1)}, u32[]{:S(2)}, u32[]{:S(2)}) collective-permute-start(bf16[216,256]{1,0:T(8,128)(2,1)S(1)} %add_convert_fusion.own_ref), channel_id=1, source_target_pairs={{0,1},{1,2},{2,3},{3,0},{4,5},{5,6},{6,7},{7,4},{8,9},{9,10},{10,1... | collective-permute-start | bytes 331784 | tf_op jit(solution)/shard_map/ppermute | solution.py:513
  117.4 6.2 %collective-permute-start.10 = (bf16[216,256]{1,0:T(8,128)(2,1)S(1)}, bf16[216,256]{1,0:T(8,128)(2,1)S(1)}, u32[]{:S(2)}, u32[]{:S(2)}) collective-permute-start(bf16[216,256]{1,0:T(8,128)(2,1)S(1)} %add_convert_fusion.own_ref), channel_id=1, source_target_pairs={{0,3},{1,0},{2,1},{3,2},{4,7},{5,4},{6,5},{7,6},{8,11},{9,8},{10,9... | collective-permute-start | bytes 331784 | tf_op jit(solution)/shard_map/ppermute | solution.py:513
  122.1 5.7 %collective-permute-start.4 = (bf16[216,256]{1,0:T(8,128)(2,1)S(1)}, bf16[216,256]{1,0:T(8,128)(2,1)S(1)}, u32[]{:S(2)}, u32[]{:S(2)}) collective-permute-start(bf16[216,256]{1,0:T(8,128)(2,1)S(1)} %add_convert_fusion.1.own_ref), channel_id=1, source_target_pairs={{0,3},{1,0},{2,1},{3,2},{4,7},{5,4},{6,5},{7,6},{8,11},{9,8},{10,9... | collective-permute-start | bytes 331784 | tf_op jit(solution)/shard_map/ppermute | solution.py:513
  123.6 6.1 %collective-permute-start.11 = (bf16[216,256]{1,0:T(8,128)(2,1)S(1)}, bf16[216,256]{1,0:T(8,128)(2,1)S(1)}, u32[]{:S(2)}, u32[]{:S(2)}) collective-permute-start(bf16[216,256]{1,0:T(8,128)(2,1)S(1)} %collective-permute-done.10.third_ref), channel_id=1, source_target_pairs={{0,3},{1,0},{2,1},{3,2},{4,7},{5,4},{6,5},{7,6},{8,11},{9,8},{10,9... | collective-permute-start | bytes 331784 | tf_op jit(solution)/shard_map/ppermute | solution.py:513
  125.9 6.8 %collective-permute-start.3 = (bf16[216,256]{1,0:T(8,128)(2,1)S(1)}, bf16[216,256]{1,0:T(8,128)(2,1)S(1)}, u32[]{:S(2)}, u32[]{:S(2)}) collective-permute-start(bf16[216,256]{1,0:T(8,128)(2,1)S(1)} %add_convert_fusion.1.own_ref), channel_id=1, source_target_pairs={{0,1},{1,2},{2,3},{3,0},{4,5},{5,6},{6,7},{7,4},{8,9},{9,10},{10,1... | collective-permute-start | bytes 331784 | tf_op jit(solution)/shard_map/ppermute | solution.py:513
  127.8 4.9 %collective-permute-start.5 = (bf16[216,256]{1,0:T(8,128)(2,1)S(1)}, bf16[216,256]{1,0:T(8,128)(2,1)S(1)}, u32[]{:S(2)}, u32[]{:S(2)}) collective-permute-start(bf16[216,256]{1,0:T(8,128)(2,1)S(1)} %collective-permute-done.4.third_ref), channel_id=1, source_target_pairs={{0,3},{1,0},{2,1},{3,2},{4,7},{5,4},{6,5},{7,6},{8,11},{9,8},{10,9... | collective-permute-start | bytes 331784 | tf_op jit(solution)/shard_map/ppermute | solution.py:513
